TPU v7x, 128 devices: a whole 4x4x4 slice. The times are simulated.
128 devices in a mesh: blk: 16 (over x_hi, z, core), grp: 8 (over y, x_lo).
Axes of the slice: x: 4 (x_hi: 2, x_lo: 2; x = x_hi * 2 + x_lo), y: 4, z: 4, core: 2. Of those that a mesh axis runs over, the one named last changes fastest.
Arguments:
- picture_vectors: bfloat16 [22528, 1152], P(('blk', 'grp')), may hold values from -0.1875 to 0.1875
- caption_vectors: bfloat16 [22528, 1152], P(('blk', 'grp')), may hold values from -0.1875 to 0.1875
- scale_exponent: float32 [1], replicated, may hold values from 2 to 2.6
- offset_term: float32 [1], replicated, may hold values from -6 to -4
Outputs:
- image_grad: float32 [22528, 1152], P(('blk', 'grp'))
- text_grad: float32 [22528, 1152], P(('blk', 'grp'))
All inputs are finite; a program needn't handle non-finite values.
Results may differ from a plain program's by a relative error of at most 0.02.
Values may be sent and summed in bfloat16 or wider, within the bound.
A program may use at most 128 MiB of HBM per device.

v0:
```python
import jax
import jax.numpy as jnp
from jax import lax
from jax.sharding import PartitionSpec as P

epsilon = 1e-06


def passed_along(block, axis, distance):
    devices = range(lax.axis_size(axis))
    route = [((i - distance) % len(devices), i) for i in devices]
    return lax.ppermute(block, axis, route)


def unit_rows(values):
    wide = values.astype(jnp.float32)
    inverse = lax.rsqrt(jnp.sum(wide * wide, axis=-1, keepdims=True) + epsilon)
    return (wide * inverse, inverse)


def match_factor(
    picture_halfwidth,
    caption_halfwidth,
    resident_entries,
    column_position,
    score_scale,
    entry_offset,
):
    match_scores = (
        score_scale
        * jnp.dot(picture_halfwidth, caption_halfwidth.T, preferred_element_type=jnp.float32)
        + entry_offset
    )
    label_polarity = jnp.where(
        resident_entries[:, None] == column_position[None, :], 1.0, -1.0
    ).astype(jnp.float32)
    return (-label_polarity * jax.nn.sigmoid(-label_polarity * match_scores) * score_scale).astype(
        jnp.bfloat16
    )


def back_project(unit, inverse, grad):
    return (grad - unit * jnp.sum(unit * grad, axis=-1, keepdims=True)) * inverse


def per_device(picture_vectors, caption_vectors, scale_exponent, offset_term):
    score_scale = jnp.exp(scale_exponent[0])
    entry_offset = offset_term[0]
    image_unit, image_inv = unit_rows(picture_vectors)
    text_unit, text_inv = unit_rows(caption_vectors)
    picture_halfwidth = image_unit.astype(jnp.bfloat16)
    caption_halfwidth = text_unit.astype(jnp.bfloat16)
    rows_dev = picture_vectors.shape[0]
    feature_count = picture_vectors.shape[1]
    blocks = lax.axis_size("blk")
    members = lax.axis_size("grp")
    block_rows = rows_dev * members
    home_index = lax.axis_index("blk")
    member = lax.axis_index("grp")
    picture_submatrix = lax.all_gather(picture_halfwidth, "grp", axis=0, tiled=True)
    resident_entries = home_index * block_rows + jnp.arange(block_rows, dtype=jnp.int32)
    image_zero = jnp.zeros((block_rows, feature_count), jnp.float32)

    def visit_block(text_slice_block, partial_value, image_acc, start_entry_index):
        column_position = start_entry_index + jnp.arange(text_slice_block.shape[0], dtype=jnp.int32)
        penalty_factor_matrix = match_factor(
            picture_submatrix,
            text_slice_block,
            resident_entries,
            column_position,
            score_scale,
            entry_offset,
        )
        image_acc = image_acc + jnp.dot(
            penalty_factor_matrix, text_slice_block, preferred_element_type=jnp.float32
        )
        partial_value = partial_value + lax.dot_general(
            penalty_factor_matrix,
            picture_submatrix,
            (((0,), (0,)), ((), ())),
            preferred_element_type=jnp.float32,
        )
        return (partial_value, image_acc)

    def first_of(anchor):
        return (anchor * members + member) * rows_dev

    own_zero = jnp.zeros((rows_dev, feature_count), jnp.float32)

    def moving_turn(turn_index, state_now):
        text_slice_block, partial_value, image_acc = state_now
        anchor = (home_index - turn_index) % blocks
        partial_value, image_acc = visit_block(
            text_slice_block, partial_value, image_acc, first_of(anchor)
        )
        text_slice_block = passed_along(text_slice_block, "blk", 1)
        partial_value = passed_along(partial_value, "blk", 1)
        return (text_slice_block, partial_value, image_acc)

    text_slice_block, partial_value, image_acc = lax.fori_loop(
        0, blocks - 1, moving_turn, (caption_halfwidth, own_zero, image_zero)
    )
    anchor = (home_index - (blocks - 1)) % blocks
    partial_value, image_acc = visit_block(
        text_slice_block, partial_value, image_acc, first_of(anchor)
    )
    text_acc = passed_along(partial_value.astype(jnp.bfloat16), "blk", 1).astype(
        partial_value.dtype
    )
    image_own = lax.psum_scatter(
        image_acc.astype(jnp.bfloat16), "grp", scatter_dimension=0, tiled=True
    ).astype(jnp.float32)
    return (
        back_project(image_unit, image_inv, image_own),
        back_project(text_unit, text_inv, text_acc),
    )


def solution(mesh):
    return jax.shard_map(
        per_device,
        mesh=mesh,
        in_specs=(P(("blk", "grp"), None), P(("blk", "grp"), None), P(), P()),
        out_specs=(P(("blk", "grp"), None), P(("blk", "grp"), None)),
        check_vma=False,
    )
```

profile of v0, /device:TPU:1, one launch (start us, length us, event | category | flops | bytes accessed | tf_op | source)
XLA Modules:
  0.0 548.1 jit_solution(14522474569847428475)
XLA Ops:
  14.1 72.6 %all-gather.2.cloned.1.call-done = bf16[1408,1152]{1,0:T(8,128)(2,1)} async-done(((bf16[176,1152]{1,0:T(8,128)(2,1)}), bf16[1408,1152]{1,0:T(8,128)(2,1)}) %all-gather.2.cloned.1.call-update) | async-done | bytes 3244048 | tf_op jit(solution)/shard_map/all_gather | solution.py:60
  86.7 356.1 %while.20 = (s32[]{:T(128)}, bf16[176,1152]{1,0:T(8,128)(2,1)S(1)}, f32[176,1152]{1,0:T(8,128)S(1)}, f32[1408,1152]{1,0:T(8,128)}, s32[]{:T(128)}, /*index=5*/s3...) while((s32[]{:T(128)}, bf16[176,1152]{1,0:T(8,128)(2,1)S(1)}, ...), condition=%wide.region_3.4_spmd.clone, body=%wide.region_2.3_spmd.clone.sunk | while | flops 1719270912 | bytes 42050356 | solution.py:100
  86.8 4.1 fusion.57
  98.0 9.6 %collective-permute-done = bf16[176,1152]{1,0:T(8,128)(2,1)S(1)} collective-permute-done((bf16[176,1152]{1,0:T(8,128)(2,1)S(1)}, bf16[176,1152]{1,0:T(8,128)(2,1)S(1)}, u32[]{:S(2)}, u32[]{:S(2)}) %collective-permute-start) | collective-permute-done | bytes 405536 | tf_op jit(solution)/shard_map/while/body/eval_jaxpr/ppermute | solution.py:12
  107.6 4.1 fusion.57
  115.3 6.7 %convolution_add_fusion.7 = f32[1408,1152]{1,0:T(8,128)} fusion(bf16[1408,176]{0,1:T(8,128)(2,1)S(1)} %fusion.57, bf16[176,1152]{1,0:T(8,128)(2,1)S(1)} %copy.11, f32[1408,1152]{1,0:T(8,128)} %get-tuple-element.386, pred[]{:T(512)S(6)} %compare.5), kind=kOutput, calls=%fused_computation.1.clone.1 | convolution fusion | flops 574193664 | bytes 13877249 | tf_op jit(solution)/shard_map/while/body/eval_jaxpr/dot_general | solution.py:74
  122.0 6.7 %collective-permute-done = bf16[176,1152]{1,0:T(8,128)(2,1)S(1)} collective-permute-done((bf16[176,1152]{1,0:T(8,128)(2,1)S(1)}, bf16[176,1152]{1,0:T(8,128)(2,1)S(1)}, u32[]{:S(2)}, u32[]{:S(2)}) %collective-permute-start) | collective-permute-done | bytes 405536 | tf_op jit(solution)/shard_map/while/body/eval_jaxpr/ppermute | solution.py:12
  128.8 4.1 fusion.57
  136.5 6.7 %convolution_add_fusion.7 = f32[1408,1152]{1,0:T(8,128)} fusion(bf16[1408,176]{0,1:T(8,128)(2,1)S(1)} %fusion.57, bf16[176,1152]{1,0:T(8,128)(2,1)S(1)} %copy.11, f32[1408,1152]{1,0:T(8,128)} %get-tuple-element.386, pred[]{:T(512)S(6)} %compare.5), kind=kOutput, calls=%fused_computation.1.clone.1 | convolution fusion | flops 574193664 | bytes 13877249 | tf_op jit(solution)/shard_map/while/body/eval_jaxpr/dot_general | solution.py:74
  143.2 6.7 %collective-permute-done = bf16[176,1152]{1,0:T(8,128)(2,1)S(1)} collective-permute-done((bf16[176,1152]{1,0:T(8,128)(2,1)S(1)}, bf16[176,1152]{1,0:T(8,128)(2,1)S(1)}, u32[]{:S(2)}, u32[]{:S(2)}) %collective-permute-start) | collective-permute-done | bytes 405536 | tf_op jit(solution)/shard_map/while/body/eval_jaxpr/ppermute | solution.py:12
  150.1 4.1 fusion.57
  157.7 6.7 %convolution_add_fusion.7 = f32[1408,1152]{1,0:T(8,128)} fusion(bf16[1408,176]{0,1:T(8,128)(2,1)S(1)} %fusion.57, bf16[176,1152]{1,0:T(8,128)(2,1)S(1)} %copy.11, f32[1408,1152]{1,0:T(8,128)} %get-tuple-element.386, pred[]{:T(512)S(6)} %compare.5), kind=kOutput, calls=%fused_computation.1.clone.1 | convolution fusion | flops 574193664 | bytes 13877249 | tf_op jit(solution)/shard_map/while/body/eval_jaxpr/dot_general | solution.py:74
  164.5 6.7 %collective-permute-done = bf16[176,1152]{1,0:T(8,128)(2,1)S(1)} collective-permute-done((bf16[176,1152]{1,0:T(8,128)(2,1)S(1)}, bf16[176,1152]{1,0:T(8,128)(2,1)S(1)}, u32[]{:S(2)}, u32[]{:S(2)}) %collective-permute-start) | collective-permute-done | bytes 405536 | tf_op jit(solution)/shard_map/while/body/eval_jaxpr/ppermute | solution.py:12
  171.3 4.1 fusion.57
  179.0 6.7 %convolution_add_fusion.7 = f32[1408,1152]{1,0:T(8,128)} fusion(bf16[1408,176]{0,1:T(8,128)(2,1)S(1)} %fusion.57, bf16[176,1152]{1,0:T(8,128)(2,1)S(1)} %copy.11, f32[1408,1152]{1,0:T(8,128)} %get-tuple-element.386, pred[]{:T(512)S(6)} %compare.5), kind=kOutput, calls=%fused_computation.1.clone.1 | convolution fusion | flops 574193664 | bytes 13877249 | tf_op jit(solution)/shard_map/while/body/eval_jaxpr/dot_general | solution.py:74
  185.7 8.9 %collective-permute-done = bf16[176,1152]{1,0:T(8,128)(2,1)S(1)} collective-permute-done((bf16[176,1152]{1,0:T(8,128)(2,1)S(1)}, bf16[176,1152]{1,0:T(8,128)(2,1)S(1)}, u32[]{:S(2)}, u32[]{:S(2)}) %collective-permute-start) | collective-permute-done | bytes 405536 | tf_op jit(solution)/shard_map/while/body/eval_jaxpr/ppermute | solution.py:12
  194.6 4.1 fusion.57
  200.2 6.7 %convolution_add_fusion.7 = f32[1408,1152]{1,0:T(8,128)} fusion(bf16[1408,176]{0,1:T(8,128)(2,1)S(1)} %fusion.57, bf16[176,1152]{1,0:T(8,128)(2,1)S(1)} %copy.11, f32[1408,1152]{1,0:T(8,128)} %get-tuple-element.386, pred[]{:T(512)S(6)} %compare.5), kind=kOutput, calls=%fused_computation.1.clone.1 | convolution fusion | flops 574193664 | bytes 13877249 | tf_op jit(solution)/shard_map/while/body/eval_jaxpr/dot_general | solution.py:74
  206.9 12.5 %collective-permute-done = bf16[176,1152]{1,0:T(8,128)(2,1)S(1)} collective-permute-done((bf16[176,1152]{1,0:T(8,128)(2,1)S(1)}, bf16[176,1152]{1,0:T(8,128)(2,1)S(1)}, u32[]{:S(2)}, u32[]{:S(2)}) %collective-permute-start) | collective-permute-done | bytes 405536 | tf_op jit(solution)/shard_map/while/body/eval_jaxpr/ppermute | solution.py:12
  219.5 4.1 fusion.57
  224.6 6.7 %convolution_add_fusion.7 = f32[1408,1152]{1,0:T(8,128)} fusion(bf16[1408,176]{0,1:T(8,128)(2,1)S(1)} %fusion.57, bf16[176,1152]{1,0:T(8,128)(2,1)S(1)} %copy.11, f32[1408,1152]{1,0:T(8,128)} %get-tuple-element.386, pred[]{:T(512)S(6)} %compare.5), kind=kOutput, calls=%fused_computation.1.clone.1 | convolution fusion | flops 574193664 | bytes 13877249 | tf_op jit(solution)/shard_map/while/body/eval_jaxpr/dot_general | solution.py:74
  231.4 12.8 %collective-permute-done = bf16[176,1152]{1,0:T(8,128)(2,1)S(1)} collective-permute-done((bf16[176,1152]{1,0:T(8,128)(2,1)S(1)}, bf16[176,1152]{1,0:T(8,128)(2,1)S(1)}, u32[]{:S(2)}, u32[]{:S(2)}) %collective-permute-start) | collective-permute-done | bytes 405536 | tf_op jit(solution)/shard_map/while/body/eval_jaxpr/ppermute | solution.py:12
  244.3 4.1 fusion.57
  249.5 6.7 %convolution_add_fusion.7 = f32[1408,1152]{1,0:T(8,128)} fusion(bf16[1408,176]{0,1:T(8,128)(2,1)S(1)} %fusion.57, bf16[176,1152]{1,0:T(8,128)(2,1)S(1)} %copy.11, f32[1408,1152]{1,0:T(8,128)} %get-tuple-element.386, pred[]{:T(512)S(6)} %compare.5), kind=kOutput, calls=%fused_computation.1.clone.1 | convolution fusion | flops 574193664 | bytes 13877249 | tf_op jit(solution)/shard_map/while/body/eval_jaxpr/dot_general | solution.py:74
  256.2 12.8 %collective-permute-done = bf16[176,1152]{1,0:T(8,128)(2,1)S(1)} collective-permute-done((bf16[176,1152]{1,0:T(8,128)(2,1)S(1)}, bf16[176,1152]{1,0:T(8,128)(2,1)S(1)}, u32[]{:S(2)}, u32[]{:S(2)}) %collective-permute-start) | collective-permute-done | bytes 405536 | tf_op jit(solution)/shard_map/while/body/eval_jaxpr/ppermute | solution.py:12
  269.1 4.1 fusion.57
  274.3 6.7 %convolution_add_fusion.7 = f32[1408,1152]{1,0:T(8,128)} fusion(bf16[1408,176]{0,1:T(8,128)(2,1)S(1)} %fusion.57, bf16[176,1152]{1,0:T(8,128)(2,1)S(1)} %copy.11, f32[1408,1152]{1,0:T(8,128)} %get-tuple-element.386, pred[]{:T(512)S(6)} %compare.5), kind=kOutput, calls=%fused_computation.1.clone.1 | convolution fusion | flops 574193664 | bytes 13877249 | tf_op jit(solution)/shard_map/while/body/eval_jaxpr/dot_general | solution.py:74
  281.0 12.8 %collective-permute-done = bf16[176,1152]{1,0:T(8,128)(2,1)S(1)} collective-permute-done((bf16[176,1152]{1,0:T(8,128)(2,1)S(1)}, bf16[176,1152]{1,0:T(8,128)(2,1)S(1)}, u32[]{:S(2)}, u32[]{:S(2)}) %collective-permute-start) | collective-permute-done | bytes 405536 | tf_op jit(solution)/shard_map/while/body/eval_jaxpr/ppermute | solution.py:12
  293.9 4.1 fusion.57
  299.1 6.7 %convolution_add_fusion.7 = f32[1408,1152]{1,0:T(8,128)} fusion(bf16[1408,176]{0,1:T(8,128)(2,1)S(1)} %fusion.57, bf16[176,1152]{1,0:T(8,128)(2,1)S(1)} %copy.11, f32[1408,1152]{1,0:T(8,128)} %get-tuple-element.386, pred[]{:T(512)S(6)} %compare.5), kind=kOutput, calls=%fused_computation.1.clone.1 | convolution fusion | flops 574193664 | bytes 13877249 | tf_op jit(solution)/shard_map/while/body/eval_jaxpr/dot_general | solution.py:74
  305.9 12.8 %collective-permute-done = bf16[176,1152]{1,0:T(8,128)(2,1)S(1)} collective-permute-done((bf16[176,1152]{1,0:T(8,128)(2,1)S(1)}, bf16[176,1152]{1,0:T(8,128)(2,1)S(1)}, u32[]{:S(2)}, u32[]{:S(2)}) %collective-permute-start) | collective-permute-done | bytes 405536 | tf_op jit(solution)/shard_map/while/body/eval_jaxpr/ppermute | solution.py:12
  318.8 4.1 fusion.57
  323.9 6.7 %convolution_add_fusion.7 = f32[1408,1152]{1,0:T(8,128)} fusion(bf16[1408,176]{0,1:T(8,128)(2,1)S(1)} %fusion.57, bf16[176,1152]{1,0:T(8,128)(2,1)S(1)} %copy.11, f32[1408,1152]{1,0:T(8,128)} %get-tuple-element.386, pred[]{:T(512)S(6)} %compare.5), kind=kOutput, calls=%fused_computation.1.clone.1 | convolution fusion | flops 574193664 | bytes 13877249 | tf_op jit(solution)/shard_map/while/body/eval_jaxpr/dot_general | solution.py:74
  330.7 12.8 %collective-permute-done = bf16[176,1152]{1,0:T(8,128)(2,1)S(1)} collective-permute-done((bf16[176,1152]{1,0:T(8,128)(2,1)S(1)}, bf16[176,1152]{1,0:T(8,128)(2,1)S(1)}, u32[]{:S(2)}, u32[]{:S(2)}) %collective-permute-start) | collective-permute-done | bytes 405536 | tf_op jit(solution)/shard_map/while/body/eval_jaxpr/ppermute | solution.py:12
  343.6 4.1 fusion.57
  348.8 6.7 %convolution_add_fusion.7 = f32[1408,1152]{1,0:T(8,128)} fusion(bf16[1408,176]{0,1:T(8,128)(2,1)S(1)} %fusion.57, bf16[176,1152]{1,0:T(8,128)(2,1)S(1)} %copy.11, f32[1408,1152]{1,0:T(8,128)} %get-tuple-element.386, pred[]{:T(512)S(6)} %compare.5), kind=kOutput, calls=%fused_computation.1.clone.1 | convolution fusion | flops 574193664 | bytes 13877249 | tf_op jit(solution)/shard_map/while/body/eval_jaxpr/dot_general | solution.py:74
  355.5 12.8 %collective-permute-done = bf16[176,1152]{1,0:T(8,128)(2,1)S(1)} collective-permute-done((bf16[176,1152]{1,0:T(8,128)(2,1)S(1)}, bf16[176,1152]{1,0:T(8,128)(2,1)S(1)}, u32[]{:S(2)}, u32[]{:S(2)}) %collective-permute-start) | collective-permute-done | bytes 405536 | tf_op jit(solution)/shard_map/while/body/eval_jaxpr/ppermute | solution.py:12
  368.4 4.1 fusion.57
  373.6 6.7 %convolution_add_fusion.7 = f32[1408,1152]{1,0:T(8,128)} fusion(bf16[1408,176]{0,1:T(8,128)(2,1)S(1)} %fusion.57, bf16[176,1152]{1,0:T(8,128)(2,1)S(1)} %copy.11, f32[1408,1152]{1,0:T(8,128)} %get-tuple-element.386, pred[]{:T(512)S(6)} %compare.5), kind=kOutput, calls=%fused_computation.1.clone.1 | convolution fusion | flops 574193664 | bytes 13877249 | tf_op jit(solution)/shard_map/while/body/eval_jaxpr/dot_general | solution.py:74
  380.3 12.8 %collective-permute-done = bf16[176,1152]{1,0:T(8,128)(2,1)S(1)} collective-permute-done((bf16[176,1152]{1,0:T(8,128)(2,1)S(1)}, bf16[176,1152]{1,0:T(8,128)(2,1)S(1)}, u32[]{:S(2)}, u32[]{:S(2)}) %collective-permute-start) | collective-permute-done | bytes 405536 | tf_op jit(solution)/shard_map/while/body/eval_jaxpr/ppermute | solution.py:12
  393.2 4.1 fusion.57
  398.4 6.7 %convolution_add_fusion.7 = f32[1408,1152]{1,0:T(8,128)} fusion(bf16[1408,176]{0,1:T(8,128)(2,1)S(1)} %fusion.57, bf16[176,1152]{1,0:T(8,128)(2,1)S(1)} %copy.11, f32[1408,1152]{1,0:T(8,128)} %get-tuple-element.386, pred[]{:T(512)S(6)} %compare.5), kind=kOutput, calls=%fused_computation.1.clone.1 | convolution fusion | flops 574193664 | bytes 13877249 | tf_op jit(solution)/shard_map/while/body/eval_jaxpr/dot_general | solution.py:74
  405.2 12.8 %collective-permute-done = bf16[176,1152]{1,0:T(8,128)(2,1)S(1)} collective-permute-done((bf16[176,1152]{1,0:T(8,128)(2,1)S(1)}, bf16[176,1152]{1,0:T(8,128)(2,1)S(1)}, u32[]{:S(2)}, u32[]{:S(2)}) %collective-permute-start) | collective-permute-done | bytes 405536 | tf_op jit(solution)/shard_map/while/body/eval_jaxpr/ppermute | solution.py:12
  418.1 4.1 fusion.57
  423.2 6.7 %convolution_add_fusion.7 = f32[1408,1152]{1,0:T(8,128)} fusion(bf16[1408,176]{0,1:T(8,128)(2,1)S(1)} %fusion.57, bf16[176,1152]{1,0:T(8,128)(2,1)S(1)} %copy.11, f32[1408,1152]{1,0:T(8,128)} %get-tuple-element.386, pred[]{:T(512)S(6)} %compare.5), kind=kOutput, calls=%fused_computation.1.clone.1 | convolution fusion | flops 574193664 | bytes 13877249 | tf_op jit(solution)/shard_map/while/body/eval_jaxpr/dot_general | solution.py:74
  430.0 12.8 %collective-permute-done = bf16[176,1152]{1,0:T(8,128)(2,1)S(1)} collective-permute-done((bf16[176,1152]{1,0:T(8,128)(2,1)S(1)}, bf16[176,1152]{1,0:T(8,128)(2,1)S(1)}, u32[]{:S(2)}, u32[]{:S(2)}) %collective-permute-start) | collective-permute-done | bytes 405536 | tf_op jit(solution)/shard_map/while/body/eval_jaxpr/ppermute | solution.py:12
  454.1 18.5 %collective-permute-done.2 = bf16[176,1152]{1,0:T(8,128)(2,1)S(1)} collective-permute-done((bf16[176,1152]{1,0:T(8,128)(2,1)S(1)}, bf16[176,1152]{1,0:T(8,128)(2,1)S(1)}, u32[]{:S(2)}, u32[]{:S(2)}) %collective-permute-start.2) | collective-permute-done | bytes 405536 | tf_op jit(solution)/shard_map/ppermute | solution.py:12
  474.0 63.7 %reduce-scatter.2.cloned.1.call-done = bf16[176,1152]{1,0:T(8,128)(2,1)} async-done(((bf16[1408,1152]{1,0:T(8,128)(2,1)}), bf16[176,1152]{1,0:T(8,128)(2,1)}) %reduce-scatter.2.cloned.1.call-update) | async-done | bytes 405520 | tf_op jit(solution)/shard_map/reduce_scatter | solution.py:110
  (170 shorter events, 54.4 us)
Async XLA Ops:
  7.2 79.5 %all-gather.2.cloned.1.call-start = ((), (), s32[]{:S(2)}) async-start(), calls=%async_computation.1 | async-start | bytes 3649536 | tf_op jit(solution)/shard_map/all_gather | solution.py:60
  10.3 527.4 %reduce-scatter.2.cloned.1.call-start = ((), (), s32[]{:S(2)}) async-start(), calls=%async_computation.2 | async-start | bytes 3649536 | tf_op jit(solution)/shard_map/reduce_scatter | solution.py:110
  86.8 4.1 copy-start.1
  91.9 15.6 %collective-permute-start.1 = (f32[176,1152]{1,0:T(8,128)S(1)}, f32[176,1152]{1,0:T(8,128)S(1)}, u32[]{:S(2)}, u32[]{:S(2)}) collective-permute-start(f32[176,1152]{1,0:T(8,128)S(1)} %convolution_add_fusion.6), channel_id=1, source_target_pairs={{120,0},{0,8},{8,16},{16,24},{24,32},{32,40},{40,48},{48,56},{56,6... | collective-permute-start | bytes 2433032 | tf_op jit(solution)/shard_map/while/body/eval_jaxpr/ppermute | solution.py:12
  94.0 13.5 %collective-permute-start = (bf16[176,1152]{1,0:T(8,128)(2,1)S(1)}, bf16[176,1152]{1,0:T(8,128)(2,1)S(1)}, u32[]{:S(2)}, u32[]{:S(2)}) collective-permute-start(bf16[176,1152]{1,0:T(8,128)(2,1)S(1)} %copy.11), channel_id=1, source_target_pairs={{120,0},{0,8},{8,16},{16,24},{24,32},{32,40},{40,48},{48,56},{56,6... | collective-permute-start | bytes 1216520 | tf_op jit(solution)/shard_map/while/body/eval_jaxpr/ppermute | solution.py:12
  107.6 4.1 copy-start.1
  112.7 16.1 %collective-permute-start.1 = (f32[176,1152]{1,0:T(8,128)S(1)}, f32[176,1152]{1,0:T(8,128)S(1)}, u32[]{:S(2)}, u32[]{:S(2)}) collective-permute-start(f32[176,1152]{1,0:T(8,128)S(1)} %convolution_add_fusion.6), channel_id=1, source_target_pairs={{120,0},{0,8},{8,16},{16,24},{24,32},{32,40},{40,48},{48,56},{56,6... | collective-permute-start | bytes 2433032 | tf_op jit(solution)/shard_map/while/body/eval_jaxpr/ppermute | solution.py:12
  115.2 13.5 %collective-permute-start = (bf16[176,1152]{1,0:T(8,128)(2,1)S(1)}, bf16[176,1152]{1,0:T(8,128)(2,1)S(1)}, u32[]{:S(2)}, u32[]{:S(2)}) collective-permute-start(bf16[176,1152]{1,0:T(8,128)(2,1)S(1)} %copy.11), channel_id=1, source_target_pairs={{120,0},{0,8},{8,16},{16,24},{24,32},{32,40},{40,48},{48,56},{56,6... | collective-permute-start | bytes 1216520 | tf_op jit(solution)/shard_map/while/body/eval_jaxpr/ppermute | solution.py:12
  128.8 4.1 copy-start.1
  133.9 16.1 %collective-permute-start.1 = (f32[176,1152]{1,0:T(8,128)S(1)}, f32[176,1152]{1,0:T(8,128)S(1)}, u32[]{:S(2)}, u32[]{:S(2)}) collective-permute-start(f32[176,1152]{1,0:T(8,128)S(1)} %convolution_add_fusion.6), channel_id=1, source_target_pairs={{120,0},{0,8},{8,16},{16,24},{24,32},{32,40},{40,48},{48,56},{56,6... | collective-permute-start | bytes 2433032 | tf_op jit(solution)/shard_map/while/body/eval_jaxpr/ppermute | solution.py:12
  136.4 13.5 %collective-permute-start = (bf16[176,1152]{1,0:T(8,128)(2,1)S(1)}, bf16[176,1152]{1,0:T(8,128)(2,1)S(1)}, u32[]{:S(2)}, u32[]{:S(2)}) collective-permute-start(bf16[176,1152]{1,0:T(8,128)(2,1)S(1)} %copy.11), channel_id=1, source_target_pairs={{120,0},{0,8},{8,16},{16,24},{24,32},{32,40},{40,48},{48,56},{56,6... | collective-permute-start | bytes 1216520 | tf_op jit(solution)/shard_map/while/body/eval_jaxpr/ppermute | solution.py:12
  150.1 4.1 copy-start.1
  155.1 16.1 %collective-permute-start.1 = (f32[176,1152]{1,0:T(8,128)S(1)}, f32[176,1152]{1,0:T(8,128)S(1)}, u32[]{:S(2)}, u32[]{:S(2)}) collective-permute-start(f32[176,1152]{1,0:T(8,128)S(1)} %convolution_add_fusion.6), channel_id=1, source_target_pairs={{120,0},{0,8},{8,16},{16,24},{24,32},{32,40},{40,48},{48,56},{56,6... | collective-permute-start | bytes 2433032 | tf_op jit(solution)/shard_map/while/body/eval_jaxpr/ppermute | solution.py:12
  157.7 13.5 %collective-permute-start = (bf16[176,1152]{1,0:T(8,128)(2,1)S(1)}, bf16[176,1152]{1,0:T(8,128)(2,1)S(1)}, u32[]{:S(2)}, u32[]{:S(2)}) collective-permute-start(bf16[176,1152]{1,0:T(8,128)(2,1)S(1)} %copy.11), channel_id=1, source_target_pairs={{120,0},{0,8},{8,16},{16,24},{24,32},{32,40},{40,48},{48,56},{56,6... | collective-permute-start | bytes 1216520 | tf_op jit(solution)/shard_map/while/body/eval_jaxpr/ppermute | solution.py:12
  171.3 4.1 copy-start.1
  176.3 18.2 %collective-permute-start.1 = (f32[176,1152]{1,0:T(8,128)S(1)}, f32[176,1152]{1,0:T(8,128)S(1)}, u32[]{:S(2)}, u32[]{:S(2)}) collective-permute-start(f32[176,1152]{1,0:T(8,128)S(1)} %convolution_add_fusion.6), channel_id=1, source_target_pairs={{120,0},{0,8},{8,16},{16,24},{24,32},{32,40},{40,48},{48,56},{56,6... | collective-permute-start | bytes 2433032 | tf_op jit(solution)/shard_map/while/body/eval_jaxpr/ppermute | solution.py:12
  178.9 15.7 %collective-permute-start = (bf16[176,1152]{1,0:T(8,128)(2,1)S(1)}, bf16[176,1152]{1,0:T(8,128)(2,1)S(1)}, u32[]{:S(2)}, u32[]{:S(2)}) collective-permute-start(bf16[176,1152]{1,0:T(8,128)(2,1)S(1)} %copy.11), channel_id=1, source_target_pairs={{120,0},{0,8},{8,16},{16,24},{24,32},{32,40},{40,48},{48,56},{56,6... | collective-permute-start | bytes 1216520 | tf_op jit(solution)/shard_map/while/body/eval_jaxpr/ppermute | solution.py:12
  194.6 4.1 copy-start.1
  199.7 19.7 %collective-permute-start.1 = (f32[176,1152]{1,0:T(8,128)S(1)}, f32[176,1152]{1,0:T(8,128)S(1)}, u32[]{:S(2)}, u32[]{:S(2)}) collective-permute-start(f32[176,1152]{1,0:T(8,128)S(1)} %convolution_add_fusion.6), channel_id=1, source_target_pairs={{120,0},{0,8},{8,16},{16,24},{24,32},{32,40},{40,48},{48,56},{56,6... | collective-permute-start | bytes 2433032 | tf_op jit(solution)/shard_map/while/body/eval_jaxpr/ppermute | solution.py:12
  200.1 19.3 %collective-permute-start = (bf16[176,1152]{1,0:T(8,128)(2,1)S(1)}, bf16[176,1152]{1,0:T(8,128)(2,1)S(1)}, u32[]{:S(2)}, u32[]{:S(2)}) collective-permute-start(bf16[176,1152]{1,0:T(8,128)(2,1)S(1)} %copy.11), channel_id=1, source_target_pairs={{120,0},{0,8},{8,16},{16,24},{24,32},{32,40},{40,48},{48,56},{56,6... | collective-permute-start | bytes 1216520 | tf_op jit(solution)/shard_map/while/body/eval_jaxpr/ppermute | solution.py:12
  219.4 4.1 copy-start.1
  224.5 19.7 %collective-permute-start.1 = (f32[176,1152]{1,0:T(8,128)S(1)}, f32[176,1152]{1,0:T(8,128)S(1)}, u32[]{:S(2)}, u32[]{:S(2)}) collective-permute-start(f32[176,1152]{1,0:T(8,128)S(1)} %convolution_add_fusion.6), channel_id=1, source_target_pairs={{120,0},{0,8},{8,16},{16,24},{24,32},{32,40},{40,48},{48,56},{56,6... | collective-permute-start | bytes 2433032 | tf_op jit(solution)/shard_map/while/body/eval_jaxpr/ppermute | solution.py:12
  224.6 19.6 %collective-permute-start = (bf16[176,1152]{1,0:T(8,128)(2,1)S(1)}, bf16[176,1152]{1,0:T(8,128)(2,1)S(1)}, u32[]{:S(2)}, u32[]{:S(2)}) collective-permute-start(bf16[176,1152]{1,0:T(8,128)(2,1)S(1)} %copy.11), channel_id=1, source_target_pairs={{120,0},{0,8},{8,16},{16,24},{24,32},{32,40},{40,48},{48,56},{56,6... | collective-permute-start | bytes 1216520 | tf_op jit(solution)/shard_map/while/body/eval_jaxpr/ppermute | solution.py:12
  244.3 4.1 copy-start.1
  249.3 19.7 %collective-permute-start.1 = (f32[176,1152]{1,0:T(8,128)S(1)}, f32[176,1152]{1,0:T(8,128)S(1)}, u32[]{:S(2)}, u32[]{:S(2)}) collective-permute-start(f32[176,1152]{1,0:T(8,128)S(1)} %convolution_add_fusion.6), channel_id=1, source_target_pairs={{120,0},{0,8},{8,16},{16,24},{24,32},{32,40},{40,48},{48,56},{56,6... | collective-permute-start | bytes 2433032 | tf_op jit(solution)/shard_map/while/body/eval_jaxpr/ppermute | solution.py:12
  249.4 19.6 %collective-permute-start = (bf16[176,1152]{1,0:T(8,128)(2,1)S(1)}, bf16[176,1152]{1,0:T(8,128)(2,1)S(1)}, u32[]{:S(2)}, u32[]{:S(2)}) collective-permute-start(bf16[176,1152]{1,0:T(8,128)(2,1)S(1)} %copy.11), channel_id=1, source_target_pairs={{120,0},{0,8},{8,16},{16,24},{24,32},{32,40},{40,48},{48,56},{56,6... | collective-permute-start | bytes 1216520 | tf_op jit(solution)/shard_map/while/body/eval_jaxpr/ppermute | solution.py:12
  269.1 4.1 copy-start.1
  274.1 19.7 %collective-permute-start.1 = (f32[176,1152]{1,0:T(8,128)S(1)}, f32[176,1152]{1,0:T(8,128)S(1)}, u32[]{:S(2)}, u32[]{:S(2)}) collective-permute-start(f32[176,1152]{1,0:T(8,128)S(1)} %convolution_add_fusion.6), channel_id=1, source_target_pairs={{120,0},{0,8},{8,16},{16,24},{24,32},{32,40},{40,48},{48,56},{56,6... | collective-permute-start | bytes 2433032 | tf_op jit(solution)/shard_map/while/body/eval_jaxpr/ppermute | solution.py:12
  274.2 19.6 %collective-permute-start = (bf16[176,1152]{1,0:T(8,128)(2,1)S(1)}, bf16[176,1152]{1,0:T(8,128)(2,1)S(1)}, u32[]{:S(2)}, u32[]{:S(2)}) collective-permute-start(bf16[176,1152]{1,0:T(8,128)(2,1)S(1)} %copy.11), channel_id=1, source_target_pairs={{120,0},{0,8},{8,16},{16,24},{24,32},{32,40},{40,48},{48,56},{56,6... | collective-permute-start | bytes 1216520 | tf_op jit(solution)/shard_map/while/body/eval_jaxpr/ppermute | solution.py:12
  293.9 4.1 copy-start.1
  299.0 19.7 %collective-permute-start.1 = (f32[176,1152]{1,0:T(8,128)S(1)}, f32[176,1152]{1,0:T(8,128)S(1)}, u32[]{:S(2)}, u32[]{:S(2)}) collective-permute-start(f32[176,1152]{1,0:T(8,128)S(1)} %convolution_add_fusion.6), channel_id=1, source_target_pairs={{120,0},{0,8},{8,16},{16,24},{24,32},{32,40},{40,48},{48,56},{56,6... | collective-permute-start | bytes 2433032 | tf_op jit(solution)/shard_map/while/body/eval_jaxpr/ppermute | solution.py:12
  299.1 19.6 %collective-permute-start = (bf16[176,1152]{1,0:T(8,128)(2,1)S(1)}, bf16[176,1152]{1,0:T(8,128)(2,1)S(1)}, u32[]{:S(2)}, u32[]{:S(2)}) collective-permute-start(bf16[176,1152]{1,0:T(8,128)(2,1)S(1)} %copy.11), channel_id=1, source_target_pairs={{120,0},{0,8},{8,16},{16,24},{24,32},{32,40},{40,48},{48,56},{56,6... | collective-permute-start | bytes 1216520 | tf_op jit(solution)/shard_map/while/body/eval_jaxpr/ppermute | solution.py:12
  323.8 19.7 %collective-permute-start.1 = (f32[176,1152]{1,0:T(8,128)S(1)}, f32[176,1152]{1,0:T(8,128)S(1)}, u32[]{:S(2)}, u32[]{:S(2)}) collective-permute-start(f32[176,1152]{1,0:T(8,128)S(1)} %convolution_add_fusion.6), channel_id=1, source_target_pairs={{120,0},{0,8},{8,16},{16,24},{24,32},{32,40},{40,48},{48,56},{56,6... | collective-permute-start | bytes 2433032 | tf_op jit(solution)/shard_map/while/body/eval_jaxpr/ppermute | solution.py:12
  323.9 19.6 %collective-permute-start = (bf16[176,1152]{1,0:T(8,128)(2,1)S(1)}, bf16[176,1152]{1,0:T(8,128)(2,1)S(1)}, u32[]{:S(2)}, u32[]{:S(2)}) collective-permute-start(bf16[176,1152]{1,0:T(8,128)(2,1)S(1)} %copy.11), channel_id=1, source_target_pairs={{120,0},{0,8},{8,16},{16,24},{24,32},{32,40},{40,48},{48,56},{56,6... | collective-permute-start | bytes 1216520 | tf_op jit(solution)/shard_map/while/body/eval_jaxpr/ppermute | solution.py:12
  343.6 4.1 copy-start.1
  348.6 19.7 %collective-permute-start.1 = (f32[176,1152]{1,0:T(8,128)S(1)}, f32[176,1152]{1,0:T(8,128)S(1)}, u32[]{:S(2)}, u32[]{:S(2)}) collective-permute-start(f32[176,1152]{1,0:T(8,128)S(1)} %convolution_add_fusion.6), channel_id=1, source_target_pairs={{120,0},{0,8},{8,16},{16,24},{24,32},{32,40},{40,48},{48,56},{56,6... | collective-permute-start | bytes 2433032 | tf_op jit(solution)/shard_map/while/body/eval_jaxpr/ppermute | solution.py:12
  348.7 19.6 %collective-permute-start = (bf16[176,1152]{1,0:T(8,128)(2,1)S(1)}, bf16[176,1152]{1,0:T(8,128)(2,1)S(1)}, u32[]{:S(2)}, u32[]{:S(2)}) collective-permute-start(bf16[176,1152]{1,0:T(8,128)(2,1)S(1)} %copy.11), channel_id=1, source_target_pairs={{120,0},{0,8},{8,16},{16,24},{24,32},{32,40},{40,48},{48,56},{56,6... | collective-permute-start | bytes 1216520 | tf_op jit(solution)/shard_map/while/body/eval_jaxpr/ppermute | solution.py:12
  373.4 19.7 %collective-permute-start.1 = (f32[176,1152]{1,0:T(8,128)S(1)}, f32[176,1152]{1,0:T(8,128)S(1)}, u32[]{:S(2)}, u32[]{:S(2)}) collective-permute-start(f32[176,1152]{1,0:T(8,128)S(1)} %convolution_add_fusion.6), channel_id=1, source_target_pairs={{120,0},{0,8},{8,16},{16,24},{24,32},{32,40},{40,48},{48,56},{56,6... | collective-permute-start | bytes 2433032 | tf_op jit(solution)/shard_map/while/body/eval_jaxpr/ppermute | solution.py:12
  373.5 19.6 %collective-permute-start = (bf16[176,1152]{1,0:T(8,128)(2,1)S(1)}, bf16[176,1152]{1,0:T(8,128)(2,1)S(1)}, u32[]{:S(2)}, u32[]{:S(2)}) collective-permute-start(bf16[176,1152]{1,0:T(8,128)(2,1)S(1)} %copy.11), channel_id=1, source_target_pairs={{120,0},{0,8},{8,16},{16,24},{24,32},{32,40},{40,48},{48,56},{56,6... | collective-permute-start | bytes 1216520 | tf_op jit(solution)/shard_map/while/body/eval_jaxpr/ppermute | solution.py:12
  393.2 4.1 copy-start.1
  398.3 19.7 %collective-permute-start.1 = (f32[176,1152]{1,0:T(8,128)S(1)}, f32[176,1152]{1,0:T(8,128)S(1)}, u32[]{:S(2)}, u32[]{:S(2)}) collective-permute-start(f32[176,1152]{1,0:T(8,128)S(1)} %convolution_add_fusion.6), channel_id=1, source_target_pairs={{120,0},{0,8},{8,16},{16,24},{24,32},{32,40},{40,48},{48,56},{56,6... | collective-permute-start | bytes 2433032 | tf_op jit(solution)/shard_map/while/body/eval_jaxpr/ppermute | solution.py:12
  398.4 19.6 %collective-permute-start = (bf16[176,1152]{1,0:T(8,128)(2,1)S(1)}, bf16[176,1152]{1,0:T(8,128)(2,1)S(1)}, u32[]{:S(2)}, u32[]{:S(2)}) collective-permute-start(bf16[176,1152]{1,0:T(8,128)(2,1)S(1)} %copy.11), channel_id=1, source_target_pairs={{120,0},{0,8},{8,16},{16,24},{24,32},{32,40},{40,48},{48,56},{56,6... | collective-permute-start | bytes 1216520 | tf_op jit(solution)/shard_map/while/body/eval_jaxpr/ppermute | solution.py:12
  423.1 19.7 %collective-permute-start.1 = (f32[176,1152]{1,0:T(8,128)S(1)}, f32[176,1152]{1,0:T(8,128)S(1)}, u32[]{:S(2)}, u32[]{:S(2)}) collective-permute-start(f32[176,1152]{1,0:T(8,128)S(1)} %convolution_add_fusion.6), channel_id=1, source_target_pairs={{120,0},{0,8},{8,16},{16,24},{24,32},{32,40},{40,48},{48,56},{56,6... | collective-permute-start | bytes 2433032 | tf_op jit(solution)/shard_map/while/body/eval_jaxpr/ppermute | solution.py:12
  423.2 19.6 %collective-permute-start = (bf16[176,1152]{1,0:T(8,128)(2,1)S(1)}, bf16[176,1152]{1,0:T(8,128)(2,1)S(1)}, u32[]{:S(2)}, u32[]{:S(2)}) collective-permute-start(bf16[176,1152]{1,0:T(8,128)(2,1)S(1)} %copy.11), channel_id=1, source_target_pairs={{120,0},{0,8},{8,16},{16,24},{24,32},{32,40},{40,48},{48,56},{56,6... | collective-permute-start | bytes 1216520 | tf_op jit(solution)/shard_map/while/body/eval_jaxpr/ppermute | solution.py:12
  442.8 4.3 copy-start
  449.9 22.6 %copy-start.4 = (bf16[176,1152]{1,0:T(8,128)(2,1)S(1)}, bf16[176,1152]{1,0:T(8,128)(2,1)}, u32[]{:S(2)}) copy-start(bf16[176,1152]{1,0:T(8,128)(2,1)} %param.7) | copy-start | bytes 1216516
  454.0 85.1 %copy-start.5 = (bf16[176,1152]{1,0:T(8,128)(2,1)S(1)}, bf16[176,1152]{1,0:T(8,128)(2,1)}, u32[]{:S(2)}) copy-start(bf16[176,1152]{1,0:T(8,128)(2,1)} %param.6) | copy-start | bytes 1216516
  454.0 18.6 %collective-permute-start.2 = (bf16[176,1152]{1,0:T(8,128)(2,1)S(1)}, bf16[176,1152]{1,0:T(8,128)(2,1)S(1)}, u32[]{:S(2)}, u32[]{:S(2)}) collective-permute-start(bf16[176,1152]{1,0:T(8,128)(2,1)S(1)} %fusion.21), channel_id=1, source_target_pairs={{120,0},{0,8},{8,16},{16,24},{24,32},{32,40},{40,48},{48,56},{56,6... | collective-permute-start | bytes 1216520 | tf_op jit(solution)/shard_map/ppermute | solution.py:12
  (6 other events, 18.5 us)
Sparse Core Ops, SparseCore 0:
  10.4 76.2 all-gather.1
  450.1 87.6 reduce-scatter.1
where the time goes:
time: 551 us; the launch traced here: 548 us
  waiting for transfers between devices  321 us (58%)
  matrix products  182 us (33%)
  between operations  15.5 us (3%)
  starting transfers between devices  14.7 us (3%)
  other arithmetic  10.5 us (2%)
    ppermute x31, waiting for transfers between devices, passed_along(): return lax.ppermute(block, axis, route)  185 us
    dot_general x16, matrix products, visit_block(): jnp.dot(penalty_factor_matrix, text_slice_block, preferred_element_type=j...  101 us
    all_gather x1, waiting for transfers between devices, per_device(): lax.all_gather(picture_halfwidth, 'grp', axis=0, tiled=True)  72.6 us
    dot_general x16, matrix products, match_factor(): jnp.dot(picture_halfwidth, caption_halfwidth.T, preferred_element_type=jn...  65.1 us
    reduce_scatter x1, waiting for transfers between devices, per_device(): lax.psum_scatter(image_acc.astype(jnp.bfloat16), 'grp', scatter_dimension...  63.7 us
    dot_general x16, matrix products, visit_block(): lax.dot_general(penalty_factor_matrix, picture_submatrix, (((0,), (0,)),...  15.6 us
    ppermute x31, starting transfers between devices, passed_along(): return lax.ppermute(block, axis, route)  14.7 us
  transfers between devices with their start and end apart: 33, of which 18 were waited for; matrix products, arithmetic and copies ran while one was open for 19% of the time, Pallas kernels for 0%

commit v1 on v0

v1 whole, which is shorter than its diff:
```python
import jax
import jax.numpy as jnp
from jax import lax
from jax.experimental import pallas as pl
from jax.experimental.pallas import tpu as pltpu
from jax.sharding import PartitionSpec as P

epsilon = 1e-06
MESH = pl.DeviceIdType.MESH
IMG, TXT = 0, 1
ROWS, D = 176, 1152
CHUNKS = ((0, 64), (64, 64), (128, 48))
FEATURES = tuple((n, min(n + 256, D)) for n in range(0, D, 256))
LANES = 8 * ROWS
PAIR = 2 * ROWS


def tiles(first, last, width=256):
    return tuple((n, min(n + width, last)) for n in range(first, last, width))


def parent(slot, chunk):
    if slot < 4:
        return 0
    return slot - 3 if slot < 7 else 4 + chunk


def step_of(slot, chunk):
    if slot < 4:
        return slot - 1
    return (slot - 4 + 1) % 3 if slot < 7 else (chunk + 2) % 3


def children(slot, chunk):
    if slot == 0:
        return (1, 2, 3)
    if slot < 4:
        return (slot + 3,)
    return (7,) if slot < 7 and chunk == slot - 4 else ()


def unit_rows(values):
    wide = values.astype(jnp.float32)
    inverse = lax.rsqrt(jnp.sum(wide * wide, axis=-1, keepdims=True) + epsilon)
    return wide * inverse, inverse


def kernel(
    scale_ref, offset_ref, picture_ref, caption_ref, image_out, text_out,
    images, texts, weights, image_part, text_part, sibling_out, sibling_in, passed_out, passed_in,
    gather_send, gather_recv, twin_send, twin_recv, back_send, back_recv, reduce_send, reduce_recv,
):
    blk = lax.axis_index("blk")
    grp = lax.axis_index("grp")
    x_hi, z, core = blk // 8, (blk // 2) % 4, blk % 2
    y, x_lo = grp // 2, grp % 2
    sibling = (blk + 1 - 2 * core, grp)
    partners = (
        (
            (blk, grp + 1 - 2 * x_lo),
            (blk, grp + 2 - 4 * (y % 2)),
            (blk + 2 - 4 * (z % 2), grp),
        ),
        (
            (blk + 8 - 16 * x_hi, grp + 1 - 2 * x_lo),
            (blk, (3 - y) * 2 + x_lo),
            (x_hi * 8 + (3 - z) * 2 + core, grp),
        ),
    )
    inputs = (picture_ref, caption_ref)
    outputs = (image_out, text_out)
    gathered = (images, texts)
    stride = (PAIR, ROWS)
    parts = (image_part, text_part)

    barrier = pltpu.get_barrier_semaphore()
    for other in (sibling,) + partners[0] + partners[1]:
        pl.semaphore_signal(barrier, inc=1, device_id=other, device_id_type=MESH)
    pl.semaphore_wait(barrier, 7)

    half_scale = jnp.exp(scale_ref[...]) * 0.5
    half_offset = offset_ref[...] * 0.5

    def gather(op, slot, chunk):
        first, count = CHUNKS[chunk]
        return pltpu.make_async_remote_copy(
            src_ref=gathered[op].at[pl.ds(parent(slot, chunk) * stride[op] + first, count)],
            dst_ref=gathered[op].at[pl.ds(slot * stride[op] + first, count)],
            send_sem=gather_send.at[op, slot, chunk],
            recv_sem=gather_recv.at[op, slot, chunk],
            device_id=partners[op][step_of(slot, chunk)],
            device_id_type=MESH,
        )

    def twin(slot):
        return pltpu.make_async_remote_copy(
            src_ref=images.at[pl.ds(slot * PAIR, ROWS)],
            dst_ref=images.at[pl.ds(slot * PAIR + ROWS, ROWS)],
            send_sem=twin_send.at[slot],
            recv_sem=twin_recv.at[slot],
            device_id=sibling,
            device_id_type=MESH,
        )

    def back(slot):
        return pltpu.make_async_remote_copy(
            src_ref=sibling_out.at[slot],
            dst_ref=sibling_in.at[slot],
            send_sem=back_send.at[slot],
            recv_sem=back_recv.at[slot],
            device_id=sibling,
            device_id_type=MESH,
        )

    def reduce(op, slot, chunk):
        first, count = CHUNKS[chunk]
        return pltpu.make_async_remote_copy(
            src_ref=passed_out.at[op, slot - 1, pl.ds(first, count)],
            dst_ref=passed_in.at[op, slot - 1, pl.ds(first, count)],
            send_sem=reduce_send.at[op, slot, chunk],
            recv_sem=reduce_recv.at[op, slot, chunk],
            device_id=partners[op][step_of(slot, chunk)],
            device_id_type=MESH,
        )

    def normalize(op):
        def rows_step(i, carry):
            rows = pl.ds(pl.multiple_of(i * 16, 16), 16)
            unit, _ = unit_rows(inputs[op][rows, :])
            gathered[op][rows, :] = unit.astype(jnp.bfloat16)
            return carry

        for first, count in CHUNKS:
            lax.fori_loop(first // 16, (first + count) // 16, rows_step, 0)
        for chunk in range(3):
            for d in range(3):
                gather(op, 1 + d, chunk).start()

    def scores(first, count, block, lanes, diagonal=False):
        def rows_step(i, carry):
            start = pl.multiple_of(first + i * block, 16)
            rows = pl.ds(start, block)
            for low, high in lanes:
                dots = lax.dot_general(
                    images[rows, :], texts[low:high, :], (((1,), (1,)), ((), ())),
                    preferred_element_type=jnp.float32,
                )
                bent = jnp.tanh(dots * half_scale + half_offset)
                if diagonal and low == 0:
                    row = start + lax.broadcasted_iota(jnp.int32, bent.shape, 0)
                    lane = lax.broadcasted_iota(jnp.int32, bent.shape, 1)
                    one = jnp.where((row == lane) & (row < ROWS), -1.0, 1.0)
                else:
                    one = 1.0
                weights[rows, low:high] = (bent + one).astype(jnp.bfloat16)
            return carry

        lax.fori_loop(0, count // block, rows_step, 0)

    def image_terms(slot):
        rows = pl.ds(slot * PAIR, PAIR)
        for low, high in FEATURES:
            terms = jnp.dot(weights[rows, :], texts[:, low:high], preferred_element_type=jnp.float32)
            image_part[slot * ROWS : (slot + 1) * ROWS, low:high] = terms[:ROWS]
            sibling_out[slot, :, low:high] = terms[ROWS:].astype(jnp.bfloat16)
        back(slot).start()

    def text_terms(first, last):
        for low, high in FEATURES:
            text_part[first:last, low:high] = lax.dot_general(
                weights[:, first:last], images[:, low:high], (((0,), (0,)), ((), ())),
                preferred_element_type=jnp.float32,
            )

    def finish(op, slot):
        if op == IMG:
            back(slot).wait_recv()
        for chunk, (first, count) in enumerate(CHUNKS):
            extra = children(slot, chunk)
            for child in extra:
                reduce(op, child, chunk).wait_recv()

            def rows_step(i, carry):
                start = pl.multiple_of(first + i * 16, 16)
                rows = pl.ds(start, 16)
                total = parts[op][pl.ds(pl.multiple_of(slot * ROWS + start, 16), 16), :]
                if op == IMG:
                    total = total + sibling_in[slot, rows, :].astype(jnp.float32)
                for child in extra:
                    total = total + passed_in[op, child - 1, rows, :].astype(jnp.float32)
                if slot:
                    passed_out[op, slot - 1, rows, :] = total.astype(jnp.bfloat16)
                else:
                    grad = total * half_scale
                    unit, inverse = unit_rows(inputs[op][rows, :])
                    along = jnp.sum(unit * grad, axis=-1, keepdims=True)
                    outputs[op][rows, :] = (grad - unit * along) * inverse
                return carry

            lax.fori_loop(0, count // 16, rows_step, 0)
            if slot:
                reduce(op, slot, chunk).start()

    normalize(IMG)
    normalize(TXT)
    twin(0).start()
    for chunk in range(3):
        for d in range(3):
            for op in (IMG, TXT):
                gather(op, 1 + d, chunk).wait_recv()
                gather(op, 4 + d, chunk).start()
    for slot in (1, 2, 3):
        twin(slot).start()
    for slot in (0, 1, 2, 3):
        twin(slot).wait_recv()
    scores(0, 4 * PAIR, 2 * PAIR, tiles(0, 640), diagonal=True)
    for chunk in range(3):
        for d in range(3):
            for op in (IMG, TXT):
                gather(op, 4 + d, chunk).wait_recv()
                if chunk == d:
                    gather(op, 7, chunk).start()
    for slot in (4, 5, 6):
        twin(slot).start()
    scores(0, 4 * PAIR, 2 * PAIR, tiles(640, 1152))
    for slot in (4, 5, 6):
        twin(slot).wait_recv()
    scores(4 * PAIR, 3 * PAIR, 528, tiles(0, 1152))
    for chunk in range(3):
        for op in (IMG, TXT):
            gather(op, 7, chunk).wait_recv()
    twin(7).start()
    scores(0, 7 * PAIR, 1232, tiles(1152, LANES))
    twin(7).wait_recv()
    scores(7 * PAIR, PAIR, PAIR, tiles(0, LANES))

    image_terms(7)
    text_terms(1152, 1408)
    finish(IMG, 7)
    finish(TXT, 7)
    image_terms(4)
    image_terms(5)
    finish(IMG, 4)
    finish(IMG, 5)
    image_terms(6)
    text_terms(896, 1152)
    finish(IMG, 6)
    finish(TXT, 6)
    text_terms(640, 896)
    finish(TXT, 5)
    finish(TXT, 4)
    image_terms(1)
    image_terms(2)
    finish(IMG, 1)
    finish(IMG, 2)
    image_terms(3)
    text_terms(384, 640)
    finish(IMG, 3)
    finish(TXT, 3)
    text_terms(128, 384)
    finish(TXT, 2)
    finish(TXT, 1)
    text_terms(0, 128)
    image_terms(0)
    finish(TXT, 0)
    finish(IMG, 0)

    for op in (IMG, TXT):
        for slot in range(1, 8):
            for chunk in range(3):
                gather(op, slot, chunk).wait_send()
                reduce(op, slot, chunk).wait_send()
    for slot in range(8):
        twin(slot).wait_send()
        back(slot).wait_send()


def per_device(picture_vectors, caption_vectors, scale_exponent, offset_term):
    wide = jax.ShapeDtypeStruct((ROWS, D), jnp.float32)
    vmem = pl.BlockSpec(memory_space=pltpu.VMEM)
    dma = pltpu.SemaphoreType.DMA
    half = jnp.bfloat16
    return pl.pallas_call(
        kernel,
        out_shape=(wide, wide),
        in_specs=[vmem] * 4,
        out_specs=(vmem, vmem),
        scratch_shapes=[
            pltpu.VMEM((8 * PAIR, D), half),
            pltpu.VMEM((LANES, D), half),
            pltpu.VMEM((8 * PAIR, LANES), half),
            pltpu.VMEM((8 * ROWS, D), jnp.float32),
            pltpu.VMEM((8 * ROWS, D), jnp.float32),
            pltpu.VMEM((8, ROWS, D), half),
            pltpu.VMEM((8, ROWS, D), half),
            pltpu.VMEM((2, 7, ROWS, D), half),
            pltpu.VMEM((2, 7, ROWS, D), half),
            dma((2, 8, 3)),
            dma((2, 8, 3)),
            dma((8,)),
            dma((8,)),
            dma((8,)),
            dma((8,)),
            dma((2, 8, 3)),
            dma((2, 8, 3)),
        ],
        compiler_params=pltpu.CompilerParams(
            collective_id=0, has_side_effects=True, vmem_limit_bytes=60 * 2**20
        ),
        cost_estimate=pl.CostEstimate(
            flops=6 * 8 * PAIR * LANES * D, bytes_accessed=6 * ROWS * D * 2, transcendentals=8 * PAIR * LANES
        ),
    )(scale_exponent.reshape(1, 1), offset_term.reshape(1, 1), picture_vectors, caption_vectors)


def solution(mesh):
    return jax.shard_map(
        per_device,
        mesh=mesh,
        in_specs=(P(("blk", "grp"), None), P(("blk", "grp"), None), P(), P()),
        out_specs=(P(("blk", "grp"), None), P(("blk", "grp"), None)),
        check_vma=False,
    )
```

time: 551 us -> 90.9 us (0.16)
  waiting for transfers between devices: 321 us -> 0 us
  matrix products: 182 us -> 0 us
  Pallas kernels: 0 us -> 85.8 us
  starting transfers between devices: 14.7 us -> 0 us
  between operations: 15.5 us -> 1.94 us
  other arithmetic: 10.5 us -> 0 us
    ppermute x31 -> x0, waiting for transfers between devices: 185 us -> none  [passed_along(): return lax.ppermute(block, axis, route)]
    dot_general x48 -> x0, matrix products: 182 us -> none  [the longest x16 101 us: visit_block(): jnp.dot(penalty_factor_matrix, text_slice_block, preferred_element_type=j...]
    pallas_call x0 -> x1, Pallas kernels: none -> 85.8 us  [per_device(): pl.pallas_call(kernel, out_shape=(wide, wide), in_specs=[vmem] * 4, out_s...]
    all_gather x1 -> x0, waiting for transfers between devices: 72.6 us -> none  [per_device(): lax.all_gather(picture_halfwidth, 'grp', axis=0, tiled=True)]
    reduce_scatter x1 -> x0, waiting for transfers between devices: 63.7 us -> none  [per_device(): lax.psum_scatter(image_acc.astype(jnp.bfloat16), 'grp', scatter_dimension...]
    ppermute x31 -> x0, starting transfers between devices: 14.7 us -> none  [passed_along(): return lax.ppermute(block, axis, route)]
  transfers between devices with their start and end apart: 33 -> 0, of which waited for: 18 -> 0; matrix products, arithmetic and copies ran while one was open for 19% -> 0% of each run, Pallas kernels for 0% -> 0%
where the time goes in v1:
time: 90.9 us; the launch traced here: 90.8 us
  Pallas kernels  85.8 us (94%)
  local copies, waits for them, and re-layouts  3.05 us (3%)
  between operations  1.94 us (2%)
    pallas_call x1, Pallas kernels, per_device(): pl.pallas_call(kernel, out_shape=(wide, wide), in_specs=[vmem] * 4, out_s...  85.8 us
    unnamed x4, local copies, waits for them, and re-layouts  3.05 us

profile of v1, /device:TPU:1, one launch (start us, length us, event | category | flops | bytes accessed | tf_op | source)
XLA Modules:
  0.0 90.8 jit_solution(5890581558411203723)
XLA Ops:
  1.9 85.8 %shard_map.59 = (f32[176,1152]{1,0:T(8,128)}, f32[176,1152]{1,0:T(8,128)}) custom-call(f32[1,1]{1,0:T(1,128)} %bitcast.2.scale_ref, f32[1,1]{1,0:T(1,128)} %bitcast.3.offset_ref, bf16[176,1152]{1,0:T(8,128)(2,1)} %picture_ref.1, bf16[176,1152]{1,0:T(8,128)(2,1)} %caption_ref.1), custom_call_target="tpu_custom_call" | custom-call | flops 27405582336 | bytes 2433024 | tf_op jit(solution)/shard_map/pallas_call | solution.py:283
  87.7 0.0 copy-start
  87.7 2.2 %copy.10 = f32[176,1152]{1,0:T(8,128)} copy(f32[176,1152]{1,0:T(8,128)} %get-tuple-element.4) | data formatting | bytes 1622016
  89.9 0.0 copy-done
  89.9 0.9 copy.11
Async XLA Ops:
  87.7 2.2 %copy-start = (f32[176,1152]{1,0:T(8,128)S(1)}, f32[176,1152]{1,0:T(8,128)}, u32[]{:S(2)}) copy-start(f32[176,1152]{1,0:T(8,128)} %get-tuple-element.5) | copy-start | bytes 2433028

commit v2 on v1

v2 whole, which is shorter than its diff:
```python
import jax
import jax.numpy as jnp
from jax import lax
from jax.experimental import pallas as pl
from jax.experimental.pallas import tpu as pltpu
from jax.sharding import PartitionSpec as P

epsilon = 1e-06
MESH = pl.DeviceIdType.MESH
IMG, TXT = 0, 1
ROWS, D = 176, 1152
CHUNKS = ((0, 64), (64, 64), (128, 48))
FEATURES = tuple((n, min(n + 256, D)) for n in range(0, D, 256))
LANES = 8 * ROWS
PAIR = 2 * ROWS
EARLY_LANES, EARLY_ROWS = 640, 1280


def place(layer, d):
    k = 0 if layer == 7 else (layer - 1) % 3
    counts = [CHUNKS[(e + k) % 3][1] for e in range(3)]
    return sum(counts[:d]), counts[d]


def source(layer, d):
    if layer < 4:
        return 0, CHUNKS[(d + layer - 1) % 3][0]
    return (layer - 3 if layer < 7 else 4), place(layer, d)[0]


def step_of(layer, d):
    return (d + (0 if layer < 4 else 1 if layer < 7 else 2)) % 3


def unit_rows(values):
    wide = values.astype(jnp.float32)
    inverse = lax.rsqrt(jnp.sum(wide * wide, axis=-1, keepdims=True) + epsilon)
    return wide * inverse, inverse


def kernel(
    scale_ref, offset_ref, picture_ref, caption_ref, image_out, text_out,
    pictures, captions, images, texts, weights, image_part, sibling_part, text_part,
    sibling_out, sibling_in, passed_out, passed_in,
    gather_send, gather_recv, twin_send, twin_recv, back_send, back_recv, reduce_send, reduce_recv, local,
):
    blk = lax.axis_index("blk")
    grp = lax.axis_index("grp")
    x_hi, z, core = blk // 8, (blk // 2) % 4, blk % 2
    y, x_lo = grp // 2, grp % 2
    sibling = (blk + 1 - 2 * core, grp)
    partners = (
        (
            (blk, grp + 1 - 2 * x_lo),
            (blk, grp + 2 - 4 * (y % 2)),
            (blk + 2 - 4 * (z % 2), grp),
        ),
        (
            (blk + 8 - 16 * x_hi, grp + 1 - 2 * x_lo),
            (blk, (3 - y) * 2 + x_lo),
            (x_hi * 8 + (3 - z) * 2 + core, grp),
        ),
    )
    inputs = (pictures, captions)
    gathered = (images, texts)
    stride = (PAIR, ROWS)
    parts = (image_part, text_part)
    BOTH = (IMG, TXT)

    loads = [
        pltpu.make_async_copy(ref, inputs[op], local.at[op])
        for op, ref in enumerate((picture_ref, caption_ref))
    ]
    for load in loads:
        load.start()
    barrier = pltpu.get_barrier_semaphore()
    for other in (sibling,) + partners[0] + partners[1]:
        pl.semaphore_signal(barrier, inc=1, device_id=other, device_id_type=MESH)

    half_scale = jnp.exp(scale_ref[...]) * 0.5
    half_offset = offset_ref[...] * 0.5

    def remote(src, dst, send, recv, device):
        return pltpu.make_async_remote_copy(
            src_ref=src, dst_ref=dst, send_sem=send, recv_sem=recv, device_id=device, device_id_type=MESH
        )

    def gather(op, layer, d):
        first, count = place(layer, d)
        origin, start = source(layer, d)
        return remote(
            gathered[op].at[pl.ds(origin * stride[op] + start, count)],
            gathered[op].at[pl.ds(layer * stride[op] + first, count)],
            gather_send.at[op, layer, d],
            gather_recv.at[op, layer, d],
            partners[op][step_of(layer, d)],
        )

    def twin(layer):
        return remote(
            images.at[pl.ds(layer * PAIR, ROWS)],
            images.at[pl.ds(layer * PAIR + ROWS, ROWS)],
            twin_send.at[layer],
            twin_recv.at[layer],
            sibling,
        )

    def back(layer):
        return remote(
            sibling_out.at[layer], sibling_in.at[layer], back_send.at[layer], back_recv.at[layer], sibling
        )

    def reduce(op, layer, d):
        rows = pl.ds(*place(layer, d))
        return remote(
            passed_out.at[op, layer - 1, rows],
            passed_in.at[op, layer - 1, rows],
            reduce_send.at[op, layer, d],
            reduce_recv.at[op, layer, d],
            partners[op][step_of(layer, d)],
        )

    def arrive(layer):
        for d in range(3):
            for op in BOTH:
                gather(op, layer, d).wait_recv()
                if layer < 4:
                    gather(op, layer + 3, d).start()
                elif layer == 4:
                    gather(op, 7, d).start()
        twin(layer).start()

    def scores(first, count, block, lanes):
        def rows_step(i, carry):
            start = pl.multiple_of(first + i * block, 16)
            rows = pl.ds(start, block)
            for low, high in lanes:
                dots = lax.dot_general(
                    images[rows, :], texts[low:high, :], (((1,), (1,)), ((), ())),
                    preferred_element_type=jnp.float32,
                )
                bent = jnp.tanh(dots * half_scale + half_offset)
                if first == 0 and low < ROWS:
                    row = start + lax.broadcasted_iota(jnp.int32, bent.shape, 0)
                    lane = low + lax.broadcasted_iota(jnp.int32, bent.shape, 1)
                    one = jnp.where((row == lane) & (row < ROWS), -1.0, 1.0)
                else:
                    one = 1.0
                weights[rows, low:high] = (bent + one).astype(jnp.bfloat16)
            return carry

        lax.fori_loop(0, count // block, rows_step, 0)

    def tiles(last):
        return ((0, 128),) + tuple((n, n + 256) for n in range(128, last, 256))

    def image_terms(layer, early=False):
        rows = pl.ds(layer * PAIR, PAIR)
        own = pl.ds(layer * ROWS, ROWS)
        split = layer < 4
        deep = pl.ds(0, EARLY_LANES) if early else pl.ds(EARLY_LANES, LANES - EARLY_LANES) if split else pl.ds(0, LANES)
        for low, high in FEATURES:
            terms = jnp.dot(weights[rows, deep], texts[deep, low:high], preferred_element_type=jnp.float32)
            mine, other = terms[:ROWS], terms[ROWS:]
            if split and not early:
                mine = mine + image_part[own, low:high]
                other = other + sibling_part[own, low:high]
            image_part[own, low:high] = mine
            if early:
                sibling_part[own, low:high] = other
            else:
                sibling_out[layer, :, low:high] = other.astype(jnp.bfloat16)
        if not early:
            back(layer).start()

    def text_terms(first, last, early=False):
        split = last <= EARLY_LANES
        deep = pl.ds(0, EARLY_ROWS) if early else pl.ds(EARLY_ROWS, 8 * PAIR - EARLY_ROWS) if split else pl.ds(0, 8 * PAIR)
        for low, high in FEATURES:
            terms = lax.dot_general(
                weights[deep, first:last], images[deep, low:high], (((0,), (0,)), ((), ())),
                preferred_element_type=jnp.float32,
            )
            if split and not early:
                terms = terms + text_part[first:last, low:high]
            text_part[first:last, low:high] = terms

    def finish(op, layer):
        child = {1: 4, 2: 5, 3: 6, 4: 7}.get(layer)
        if op == IMG:
            back(layer).wait_recv()
        for d in range(3):
            first, count = place(layer, d)
            rows = pl.ds(first, count)
            total = parts[op][pl.ds(layer * ROWS + first, count), :]
            if op == IMG:
                total = total + sibling_in[layer, rows, :].astype(jnp.float32)
            if child is not None:
                reduce(op, child, d).wait_recv()
                total = total + passed_in[op, child - 1, rows, :].astype(jnp.float32)
            passed_out[op, layer - 1, rows, :] = total.astype(jnp.bfloat16)
            reduce(op, layer, d).start()

    def store(op, chunk):
        rows = pl.ds(*CHUNKS[chunk])
        return pltpu.make_async_copy(
            parts[op].at[rows], (image_out, text_out)[op].at[rows], local.at[2 + 3 * op + chunk]
        )

    def finish_own(op):
        if op == IMG:
            back(0).wait_recv()
        for chunk, (first, count) in enumerate(CHUNKS):
            rows = pl.ds(first, count)
            total = parts[op][rows, :]
            if op == IMG:
                total = total + sibling_in[0, rows, :].astype(jnp.float32)
            for d in range(3):
                child = 1 + (chunk - d) % 3
                reduce(op, child, d).wait_recv()
                total = total + passed_in[op, child - 1, pl.ds(*place(child, d)), :].astype(jnp.float32)
            grad = total * half_scale
            unit, inverse = unit_rows(inputs[op][rows, :])
            along = jnp.sum(unit * grad, axis=-1, keepdims=True)
            parts[op][rows, :] = (grad - unit * along) * inverse
            store(op, chunk).start()

    for op in BOTH:
        loads[op].wait()
        for first, count in CHUNKS:
            rows = pl.ds(first, count)
            unit, _ = unit_rows(inputs[op][rows, :])
            gathered[op][rows, :] = unit.astype(jnp.bfloat16)
    pl.semaphore_wait(barrier, 7)
    for layer in (1, 2, 3):
        for d in range(3):
            for op in BOTH:
                gather(op, layer, d).start()
    twin(0).start()

    arrive(1)
    twin(0).wait_recv()
    twin(1).wait_recv()
    scores(0, 2 * PAIR, 2 * PAIR, tiles(128))
    arrive(2)
    scores(0, 2 * PAIR, 2 * PAIR, ((128, 384),))
    twin(2).wait_recv()
    scores(2 * PAIR, PAIR, PAIR, tiles(384))
    arrive(3)
    scores(0, 3 * PAIR, 528, ((384, 640),))
    twin(3).wait_recv()
    scores(3 * PAIR, PAIR, PAIR, tiles(640))
    for layer in (0, 1):
        image_terms(layer, early=True)
    arrive(4)
    for first in (0, 128, 384):
        text_terms(first, first + (256 if first else 128), early=True)
    for layer in (2, 3):
        image_terms(layer, early=True)
    twin(4).wait_recv()
    scores(4 * PAIR, PAIR, PAIR, tiles(640))
    arrive(5)
    scores(0, 5 * PAIR, 880, ((640, 896),))
    twin(5).wait_recv()
    scores(5 * PAIR, PAIR, PAIR, tiles(896))
    arrive(6)
    scores(0, 6 * PAIR, 704, ((896, 1152),))
    twin(6).wait_recv()
    scores(6 * PAIR, PAIR, PAIR, tiles(1152))
    arrive(7)
    scores(0, 7 * PAIR, 1232, ((1152, LANES),))
    twin(7).wait_recv()
    scores(7 * PAIR, PAIR, PAIR, tiles(LANES))

    image_terms(7)
    text_terms(1152, 1408)
    finish(IMG, 7)
    finish(TXT, 7)
    image_terms(6)
    text_terms(896, 1152)
    finish(IMG, 6)
    finish(TXT, 6)
    image_terms(5)
    text_terms(640, 896)
    finish(IMG, 5)
    finish(TXT, 5)
    image_terms(4)
    finish(TXT, 4)
    finish(IMG, 4)
    image_terms(3)
    text_terms(384, 640)
    finish(IMG, 3)
    finish(TXT, 3)
    image_terms(2)
    text_terms(128, 384)
    finish(IMG, 2)
    finish(TXT, 2)
    image_terms(1)
    finish(TXT, 1)
    finish(IMG, 1)
    image_terms(0)
    text_terms(0, 128)
    finish_own(IMG)
    finish_own(TXT)

    for op in BOTH:
        for chunk in range(3):
            store(op, chunk).wait()
        for layer in range(1, 8):
            for d in range(3):
                gather(op, layer, d).wait_send()
                reduce(op, layer, d).wait_send()
    for layer in range(8):
        twin(layer).wait_send()
        back(layer).wait_send()


def per_device(picture_vectors, caption_vectors, scale_exponent, offset_term):
    wide = jax.ShapeDtypeStruct((ROWS, D), jnp.float32)
    vmem = pl.BlockSpec(memory_space=pltpu.VMEM)
    hbm = pl.BlockSpec(memory_space=pl.ANY)
    dma = pltpu.SemaphoreType.DMA
    half = jnp.bfloat16
    return pl.pallas_call(
        kernel,
        out_shape=(wide, wide),
        in_specs=[vmem, vmem, hbm, hbm],
        out_specs=(hbm, hbm),
        scratch_shapes=[
            pltpu.VMEM((ROWS, D), half),
            pltpu.VMEM((ROWS, D), half),
            pltpu.VMEM((8 * PAIR, D), half),
            pltpu.VMEM((LANES, D), half),
            pltpu.VMEM((8 * PAIR, LANES), half),
            pltpu.VMEM((8 * ROWS, D), jnp.float32),
            pltpu.VMEM((4 * ROWS, D), jnp.float32),
            pltpu.VMEM((8 * ROWS, D), jnp.float32),
            pltpu.VMEM((8, ROWS, D), half),
            pltpu.VMEM((8, ROWS, D), half),
            pltpu.VMEM((2, 7, ROWS, D), half),
            pltpu.VMEM((2, 7, ROWS, D), half),
            dma((2, 8, 3)),
            dma((2, 8, 3)),
            dma((8,)),
            dma((8,)),
            dma((8,)),
            dma((8,)),
            dma((2, 8, 3)),
            dma((2, 8, 3)),
            dma((8,)),
        ],
        compiler_params=pltpu.CompilerParams(
            collective_id=0, has_side_effects=True, vmem_limit_bytes=60 * 2**20
        ),
        cost_estimate=pl.CostEstimate(
            flops=6 * 8 * PAIR * LANES * D, bytes_accessed=6 * ROWS * D * 2, transcendentals=8 * PAIR * LANES
        ),
    )(scale_exponent.reshape(1, 1), offset_term.reshape(1, 1), picture_vectors, caption_vectors)


def solution(mesh):
    return jax.shard_map(
        per_device,
        mesh=mesh,
        in_specs=(P(("blk", "grp"), None), P(("blk", "grp"), None), P(), P()),
        out_specs=(P(("blk", "grp"), None), P(("blk", "grp"), None)),
        check_vma=False,
    )
```

time: 90.9 us -> 76.5 us (0.84)
  Pallas kernels: 85.8 us -> 71.4 us
    pallas_call x1, Pallas kernels: 85.8 us -> 71.4 us  [per_device(): pl.pallas_call(kernel, out_shape=(wide, wide), in_specs=[vmem, vmem, hbm,...]
where the time goes in v2:
time: 76.5 us; the launch traced here: 76.3 us
  Pallas kernels  71.4 us (93%)
  local copies, waits for them, and re-layouts  3.05 us (4%)
  between operations  1.94 us (3%)
    pallas_call x1, Pallas kernels, per_device(): pl.pallas_call(kernel, out_shape=(wide, wide), in_specs=[vmem, vmem, hbm,...  71.4 us
    unnamed x4, local copies, waits for them, and re-layouts  3.05 us

profile of v2, /device:TPU:1, one launch (start us, length us, event | category | flops | bytes accessed | tf_op | source)
XLA Modules:
  0.0 76.3 jit_solution(4757687143409482910)
XLA Ops:
  1.9 71.4 %shard_map.59 = (f32[176,1152]{1,0:T(8,128)}, f32[176,1152]{1,0:T(8,128)}) custom-call(f32[1,1]{1,0:T(1,128)} %bitcast.2.scale_ref, f32[1,1]{1,0:T(1,128)} %bitcast.3.offset_ref, bf16[176,1152]{1,0:T(8,128)(2,1)} %picture_ref.1, bf16[176,1152]{1,0:T(8,128)(2,1)} %caption_ref.1), custom_call_target="tpu_custom_call" | custom-call | flops 27405582336 | bytes 2433024 | tf_op jit(solution)/shard_map/pallas_call | solution.py:324
  73.3 0.0 copy-start
  73.3 2.2 %copy.10 = f32[176,1152]{1,0:T(8,128)} copy(f32[176,1152]{1,0:T(8,128)} %get-tuple-element.4) | data formatting | bytes 1622016
  75.4 0.0 copy-done
  75.5 0.9 %copy.11 = f32[176,1152]{1,0:T(8,128)} copy(f32[176,1152]{1,0:T(8,128)S(1)} %copy-done) | data formatting | bytes 1622016
Async XLA Ops:
  73.3 2.2 %copy-start = (f32[176,1152]{1,0:T(8,128)S(1)}, f32[176,1152]{1,0:T(8,128)}, u32[]{:S(2)}) copy-start(f32[176,1152]{1,0:T(8,128)} %get-tuple-element.5) | copy-start | bytes 2433028

commit v3 on v2

--- a/solution.py
+++ b/solution.py
@@ -13,7 +13,6 @@
 FEATURES = tuple((n, min(n + 256, D)) for n in range(0, D, 256))
 LANES = 8 * ROWS
 PAIR = 2 * ROWS
-EARLY_LANES, EARLY_ROWS = 640, 1280
 
 
 def place(layer, d):
@@ -154,34 +153,38 @@
     def tiles(last):
         return ((0, 128),) + tuple((n, n + 256) for n in range(128, last, 256))
 
-    def image_terms(layer, early=False):
+    image_depth, text_depth = {}, {}
+
+    def image_terms(layer, depth=LANES):
+        begun = image_depth.get(layer, 0)
+        image_depth[layer] = depth
         rows = pl.ds(layer * PAIR, PAIR)
         own = pl.ds(layer * ROWS, ROWS)
-        split = layer < 4
-        deep = pl.ds(0, EARLY_LANES) if early else pl.ds(EARLY_LANES, LANES - EARLY_LANES) if split else pl.ds(0, LANES)
+        deep = pl.ds(begun, depth - begun)
         for low, high in FEATURES:
             terms = jnp.dot(weights[rows, deep], texts[deep, low:high], preferred_element_type=jnp.float32)
             mine, other = terms[:ROWS], terms[ROWS:]
-            if split and not early:
+            if begun:
                 mine = mine + image_part[own, low:high]
                 other = other + sibling_part[own, low:high]
             image_part[own, low:high] = mine
-            if early:
+            if depth < LANES:
                 sibling_part[own, low:high] = other
             else:
                 sibling_out[layer, :, low:high] = other.astype(jnp.bfloat16)
-        if not early:
+        if depth == LANES:
             back(layer).start()
 
-    def text_terms(first, last, early=False):
-        split = last <= EARLY_LANES
-        deep = pl.ds(0, EARLY_ROWS) if early else pl.ds(EARLY_ROWS, 8 * PAIR - EARLY_ROWS) if split else pl.ds(0, 8 * PAIR)
+    def text_terms(first, last, depth=8 * PAIR):
+        begun = text_depth.get(first, 0)
+        text_depth[first] = depth
+        deep = pl.ds(begun, depth - begun)
         for low, high in FEATURES:
             terms = lax.dot_general(
                 weights[deep, first:last], images[deep, low:high], (((0,), (0,)), ((), ())),
                 preferred_element_type=jnp.float32,
             )
-            if split and not early:
+            if begun:
                 terms = terms + text_part[first:last, low:high]
             text_part[first:last, low:high] = terms
 
@@ -219,7 +222,7 @@
                 child = 1 + (chunk - d) % 3
                 reduce(op, child, d).wait_recv()
                 total = total + passed_in[op, child - 1, pl.ds(*place(child, d)), :].astype(jnp.float32)
-            grad = total * half_scale
+            grad = total
             unit, inverse = unit_rows(inputs[op][rows, :])
             along = jnp.sum(unit * grad, axis=-1, keepdims=True)
             parts[op][rows, :] = (grad - unit * along) * inverse
@@ -238,68 +241,83 @@
                 gather(op, layer, d).start()
     twin(0).start()
 
+    twin(0).wait_recv()
     arrive(1)
-    twin(0).wait_recv()
+    arrive(2)
+    twin(2).wait_recv()
     twin(1).wait_recv()
-    scores(0, 2 * PAIR, 2 * PAIR, tiles(128))
-    arrive(2)
-    scores(0, 2 * PAIR, 2 * PAIR, ((128, 384),))
-    twin(2).wait_recv()
+    arrive(3)
+    scores(0, PAIR, PAIR, ((384, 640),))
+    scores(0, PAIR, PAIR, ((128, 384),))
+    scores(PAIR, PAIR, PAIR, tiles(128))
+    scores(PAIR, PAIR, PAIR, ((384, 640),))
+    scores(0, PAIR, PAIR, tiles(128))
+    twin(3).wait_recv()
     scores(2 * PAIR, PAIR, PAIR, tiles(384))
-    arrive(3)
-    scores(0, 3 * PAIR, 528, ((384, 640),))
-    twin(3).wait_recv()
+    scores(2 * PAIR, PAIR, PAIR, ((384, 640),))
+    arrive(4)
     scores(3 * PAIR, PAIR, PAIR, tiles(640))
-    for layer in (0, 1):
-        image_terms(layer, early=True)
-    arrive(4)
-    for first in (0, 128, 384):
-        text_terms(first, first + (256 if first else 128), early=True)
-    for layer in (2, 3):
-        image_terms(layer, early=True)
+    text_terms(384, 640, 1280)
     twin(4).wait_recv()
     scores(4 * PAIR, PAIR, PAIR, tiles(640))
     arrive(5)
-    scores(0, 5 * PAIR, 880, ((640, 896),))
+    scores(PAIR, PAIR, PAIR, ((640, 896),))
+    scores(3 * PAIR, PAIR, PAIR, ((640, 896),))
+    image_terms(4, 640)
+    scores(2 * PAIR, PAIR, PAIR, ((640, 896),))
+    scores(0, PAIR, PAIR, ((640, 896),))
+    scores(4 * PAIR, PAIR, PAIR, ((640, 896),))
     twin(5).wait_recv()
     scores(5 * PAIR, PAIR, PAIR, tiles(896))
     arrive(6)
-    scores(0, 6 * PAIR, 704, ((896, 1152),))
+    scores(3 * PAIR, PAIR, PAIR, ((896, 1152),))
+    scores(2 * PAIR, PAIR, PAIR, ((896, 1152),))
+    scores(PAIR, PAIR, PAIR, ((896, 1152),))
+    arrive(7)
+    scores(0, PAIR, PAIR, ((896, 1152),))
+    scores(5 * PAIR, PAIR, PAIR, ((896, 1152),))
+    scores(5 * PAIR, PAIR, PAIR, ((1152, 1408),))
+    scores(PAIR, PAIR, PAIR, ((1152, 1408),))
+    scores(3 * PAIR, PAIR, PAIR, ((1152, 1408),))
+    scores(4 * PAIR, PAIR, PAIR, ((1152, 1408),))
     twin(6).wait_recv()
+    image_terms(5)
+    twin(7).wait_recv()
+    scores(7 * PAIR, PAIR, PAIR, ((1152, 1408),))
+    scores(2 * PAIR, PAIR, PAIR, ((1152, 1408),))
+    scores(4 * PAIR, PAIR, PAIR, ((896, 1152),))
+    scores(7 * PAIR, PAIR, PAIR, tiles(1152))
+    finish(IMG, 5)
+    image_terms(7)
+    scores(0, PAIR, PAIR, ((1152, 1408),))
+    scores(6 * PAIR, PAIR, PAIR, ((1152, 1408),))
+    text_terms(1152, 1408)
+    finish(TXT, 7)
     scores(6 * PAIR, PAIR, PAIR, tiles(1152))
-    arrive(7)
-    scores(0, 7 * PAIR, 1232, ((1152, LANES),))
-    twin(7).wait_recv()
-    scores(7 * PAIR, PAIR, PAIR, tiles(LANES))
-
-    image_terms(7)
-    text_terms(1152, 1408)
     finish(IMG, 7)
-    finish(TXT, 7)
-    image_terms(6)
     text_terms(896, 1152)
-    finish(IMG, 6)
     finish(TXT, 6)
-    image_terms(5)
+    image_terms(4)
     text_terms(640, 896)
-    finish(IMG, 5)
-    finish(TXT, 5)
-    image_terms(4)
     finish(TXT, 4)
     finish(IMG, 4)
+    image_terms(6)
+    scores(PAIR, PAIR, PAIR, ((128, 384),))
+    finish(TXT, 5)
+    image_terms(2)
+    finish(IMG, 6)
+    text_terms(384, 640)
+    image_terms(1)
+    finish(IMG, 2)
+    finish(TXT, 3)
+    text_terms(128, 384)
+    finish(IMG, 1)
+    finish(TXT, 2)
     image_terms(3)
-    text_terms(384, 640)
+    finish(TXT, 1)
     finish(IMG, 3)
-    finish(TXT, 3)
-    image_terms(2)
-    text_terms(128, 384)
-    finish(IMG, 2)
-    finish(TXT, 2)
-    image_terms(1)
-    finish(TXT, 1)
-    finish(IMG, 1)
+    text_terms(0, 128)
     image_terms(0)
-    text_terms(0, 128)
     finish_own(IMG)
     finish_own(TXT)
 
@@ -321,7 +339,7 @@
     hbm = pl.BlockSpec(memory_space=pl.ANY)
     dma = pltpu.SemaphoreType.DMA
     half = jnp.bfloat16
-    return pl.pallas_call(
+    image_sum, text_sum = pl.pallas_call(
         kernel,
         out_shape=(wide, wide),
         in_specs=[vmem, vmem, hbm, hbm],
@@ -333,7 +351,7 @@
             pltpu.VMEM((LANES, D), half),
             pltpu.VMEM((8 * PAIR, LANES), half),
             pltpu.VMEM((8 * ROWS, D), jnp.float32),
-            pltpu.VMEM((4 * ROWS, D), jnp.float32),
+            pltpu.VMEM((5 * ROWS, D), jnp.float32),
             pltpu.VMEM((8 * ROWS, D), jnp.float32),
             pltpu.VMEM((8, ROWS, D), half),
             pltpu.VMEM((8, ROWS, D), half),
@@ -357,6 +375,8 @@
         ),
     )(scale_exponent.reshape(1, 1), offset_term.reshape(1, 1), picture_vectors, caption_vectors)
 
+    half_scale = jnp.exp(scale_exponent) * 0.5
+    return image_sum * half_scale, text_sum * half_scale
 
 def solution(mesh):
     return jax.shard_map(

time: 76.5 us -> 75.8 us (level)
  local copies, waits for them, and re-layouts: 3.05 us -> 0 us
  other arithmetic: 0 us -> 2.65 us
    unnamed x4 -> x0, local copies, waits for them, and re-layouts: 3.05 us -> none
    mul x0 -> x1, other arithmetic: none -> 2.65 us  [per_device(): return (image_sum * half_scale, text_sum * half_scale)]
where the time goes in v3:
time: 75.8 us; the launch traced here: 75.6 us
  Pallas kernels  71 us (94%)
  other arithmetic  2.65 us (3%)
  between operations  1.97 us (3%)
    pallas_call x1, Pallas kernels, per_device(): pl.pallas_call(kernel, out_shape=(wide, wide), in_specs=[vmem, vmem, hbm,...  71 us
    mul x1, other arithmetic, per_device(): return (image_sum * half_scale, text_sum * half_scale)  2.65 us

profile of v3, /device:TPU:1, one launch (start us, length us, event | category | flops | bytes accessed | tf_op | source)
XLA Modules:
  0.0 75.6 jit_solution(11140757963939558762)
XLA Ops:
  2.0 71.0 %shard_map.59 = (f32[176,1152]{1,0:T(8,128)}, f32[176,1152]{1,0:T(8,128)}) custom-call(f32[1,1]{1,0:T(1,128)} %bitcast.3.scale_ref, f32[1,1]{1,0:T(1,128)} %bitcast.4.offset_ref, bf16[176,1152]{1,0:T(8,128)(2,1)} %picture_ref.1, bf16[176,1152]{1,0:T(8,128)(2,1)} %caption_ref.1), custom_call_target="tpu_custom_call" | custom-call | flops 27405582336 | bytes 2433024 | tf_op jit(solution)/shard_map/pallas_call | solution.py:342
  73.0 2.7 %broadcast_multiply_fusion = (f32[176,1152]{1,0:T(8,128)}, f32[176,1152]{1,0:T(8,128)}) fusion(f32[176,1152]{1,0:T(8,128)} %get-tuple-element.5, f32[]{:T(128)} %bitcast.2, f32[176,1152]{1,0:T(8,128)} %get-tuple-element.4), kind=kLoop, calls=%fused_computation | loop fusion | flops 405504 | bytes 3244036 | tf_op jit(solution)/shard_map/mul | solution.py:379

commit v4 on v3

--- a/solution.py
+++ b/solution.py
@@ -13,6 +13,7 @@
 FEATURES = tuple((n, min(n + 256, D)) for n in range(0, D, 256))
 LANES = 8 * ROWS
 PAIR = 2 * ROWS
+LAST = (1, 2)
 
 
 def place(layer, d):
@@ -210,7 +211,7 @@
             parts[op].at[rows], (image_out, text_out)[op].at[rows], local.at[2 + 3 * op + chunk]
         )
 
-    def finish_own(op):
+    def gather_own(op):
         if op == IMG:
             back(0).wait_recv()
         for chunk, (first, count) in enumerate(CHUNKS):
@@ -220,10 +221,18 @@
                 total = total + sibling_in[0, rows, :].astype(jnp.float32)
             for d in range(3):
                 child = 1 + (chunk - d) % 3
-                reduce(op, child, d).wait_recv()
-                total = total + passed_in[op, child - 1, pl.ds(*place(child, d)), :].astype(jnp.float32)
-            grad = total
+                if child != LAST[op]:
+                    reduce(op, child, d).wait_recv()
+                    total = total + passed_in[op, child - 1, pl.ds(*place(child, d)), :].astype(jnp.float32)
+            parts[op][rows, :] = total
+
+    def finish_own(op):
+        for chunk, (first, count) in enumerate(CHUNKS):
+            rows = pl.ds(first, count)
+            d = (chunk - LAST[op] + 1) % 3
             unit, inverse = unit_rows(inputs[op][rows, :])
+            reduce(op, LAST[op], d).wait_recv()
+            grad = parts[op][rows, :] + passed_in[op, LAST[op] - 1, pl.ds(*place(LAST[op], d)), :].astype(jnp.float32)
             along = jnp.sum(unit * grad, axis=-1, keepdims=True)
             parts[op][rows, :] = (grad - unit * along) * inverse
             store(op, chunk).start()
@@ -244,80 +253,83 @@
     twin(0).wait_recv()
     arrive(1)
     arrive(2)
+    twin(1).wait_recv()
+    scores(0, PAIR, PAIR, tiles(128))
+    scores(PAIR, PAIR, PAIR, tiles(128))
+    arrive(3)
+    scores(0, PAIR, PAIR, ((128, 384),))
+    scores(0, PAIR, PAIR, ((384, 640),))
+    scores(PAIR, PAIR, PAIR, ((128, 384),))
     twin(2).wait_recv()
-    twin(1).wait_recv()
-    arrive(3)
-    scores(0, PAIR, PAIR, ((384, 640),))
-    scores(0, PAIR, PAIR, ((128, 384),))
-    scores(PAIR, PAIR, PAIR, tiles(128))
-    scores(PAIR, PAIR, PAIR, ((384, 640),))
-    scores(0, PAIR, PAIR, tiles(128))
-    twin(3).wait_recv()
     scores(2 * PAIR, PAIR, PAIR, tiles(384))
     scores(2 * PAIR, PAIR, PAIR, ((384, 640),))
+    image_terms(2, 640)
     arrive(4)
+    scores(PAIR, PAIR, PAIR, ((384, 640),))
+    text_terms(128, 384, 1024)
+    twin(3).wait_recv()
     scores(3 * PAIR, PAIR, PAIR, tiles(640))
-    text_terms(384, 640, 1280)
+    image_terms(3, 640)
+    arrive(5)
     twin(4).wait_recv()
+    scores(2 * PAIR, PAIR, PAIR, ((640, 896),))
     scores(4 * PAIR, PAIR, PAIR, tiles(640))
-    arrive(5)
+    scores(4 * PAIR, PAIR, PAIR, ((640, 896),))
+    scores(3 * PAIR, PAIR, PAIR, ((640, 896),))
     scores(PAIR, PAIR, PAIR, ((640, 896),))
-    scores(3 * PAIR, PAIR, PAIR, ((640, 896),))
-    image_terms(4, 640)
-    scores(2 * PAIR, PAIR, PAIR, ((640, 896),))
     scores(0, PAIR, PAIR, ((640, 896),))
-    scores(4 * PAIR, PAIR, PAIR, ((640, 896),))
     twin(5).wait_recv()
     scores(5 * PAIR, PAIR, PAIR, tiles(896))
     arrive(6)
+    scores(4 * PAIR, PAIR, PAIR, ((896, 1152),))
+    arrive(7)
+    scores(5 * PAIR, PAIR, PAIR, ((1152, 1408),))
+    scores(0, PAIR, PAIR, ((896, 1152),))
+    scores(2 * PAIR, PAIR, PAIR, ((896, 1152),))
+    scores(2 * PAIR, PAIR, PAIR, ((1152, 1408),))
+    scores(PAIR, PAIR, PAIR, ((1152, 1408),))
+    scores(0, PAIR, PAIR, ((1152, 1408),))
+    scores(3 * PAIR, PAIR, PAIR, ((1152, 1408),))
+    twin(6).wait_recv()
+    scores(6 * PAIR, PAIR, PAIR, tiles(1152))
+    scores(5 * PAIR, PAIR, PAIR, ((896, 1152),))
+    scores(6 * PAIR, PAIR, PAIR, ((1152, 1408),))
+    image_terms(6)
+    twin(7).wait_recv()
+    scores(4 * PAIR, PAIR, PAIR, ((1152, 1408),))
+    scores(7 * PAIR, PAIR, PAIR, ((1152, 1408),))
+    scores(PAIR, PAIR, PAIR, ((896, 1152),))
+    text_terms(1152, 1408)
+    finish(IMG, 6)
+    scores(7 * PAIR, PAIR, PAIR, tiles(1152))
+    finish(TXT, 7)
+    image_terms(7)
     scores(3 * PAIR, PAIR, PAIR, ((896, 1152),))
-    scores(2 * PAIR, PAIR, PAIR, ((896, 1152),))
-    scores(PAIR, PAIR, PAIR, ((896, 1152),))
-    arrive(7)
-    scores(0, PAIR, PAIR, ((896, 1152),))
-    scores(5 * PAIR, PAIR, PAIR, ((896, 1152),))
-    scores(5 * PAIR, PAIR, PAIR, ((1152, 1408),))
-    scores(PAIR, PAIR, PAIR, ((1152, 1408),))
-    scores(3 * PAIR, PAIR, PAIR, ((1152, 1408),))
-    scores(4 * PAIR, PAIR, PAIR, ((1152, 1408),))
-    twin(6).wait_recv()
+    image_terms(3)
+    text_terms(896, 1152)
+    finish(IMG, 7)
+    finish(TXT, 6)
     image_terms(5)
-    twin(7).wait_recv()
-    scores(7 * PAIR, PAIR, PAIR, ((1152, 1408),))
-    scores(2 * PAIR, PAIR, PAIR, ((1152, 1408),))
-    scores(4 * PAIR, PAIR, PAIR, ((896, 1152),))
-    scores(7 * PAIR, PAIR, PAIR, tiles(1152))
-    finish(IMG, 5)
-    image_terms(7)
-    scores(0, PAIR, PAIR, ((1152, 1408),))
-    scores(6 * PAIR, PAIR, PAIR, ((1152, 1408),))
-    text_terms(1152, 1408)
-    finish(TXT, 7)
-    scores(6 * PAIR, PAIR, PAIR, tiles(1152))
-    finish(IMG, 7)
-    text_terms(896, 1152)
-    finish(TXT, 6)
-    image_terms(4)
+    finish(IMG, 3)
     text_terms(640, 896)
     finish(TXT, 4)
+    finish(TXT, 5)
+    image_terms(4)
+    finish(IMG, 5)
+    text_terms(384, 640)
+    image_terms(2)
+    finish(TXT, 3)
     finish(IMG, 4)
-    image_terms(6)
-    scores(PAIR, PAIR, PAIR, ((128, 384),))
-    finish(TXT, 5)
-    image_terms(2)
-    finish(IMG, 6)
-    text_terms(384, 640)
     image_terms(1)
+    text_terms(128, 384)
+    finish(TXT, 1)
     finish(IMG, 2)
-    finish(TXT, 3)
-    text_terms(128, 384)
+    finish(TXT, 2)
     finish(IMG, 1)
-    finish(TXT, 2)
-    image_terms(3)
-    finish(TXT, 1)
-    finish(IMG, 3)
+    image_terms(0)
     text_terms(0, 128)
-    image_terms(0)
+    gather_own(IMG)
+    gather_own(TXT)
     finish_own(IMG)
     finish_own(TXT)
 
@@ -351,7 +363,7 @@
             pltpu.VMEM((LANES, D), half),
             pltpu.VMEM((8 * PAIR, LANES), half),
             pltpu.VMEM((8 * ROWS, D), jnp.float32),
-            pltpu.VMEM((5 * ROWS, D), jnp.float32),
+            pltpu.VMEM((4 * ROWS, D), jnp.float32),
             pltpu.VMEM((8 * ROWS, D), jnp.float32),
             pltpu.VMEM((8, ROWS, D), half),
             pltpu.VMEM((8, ROWS, D), half),
@@ -368,7 +380,7 @@
             dma((8,)),
         ],
         compiler_params=pltpu.CompilerParams(
-            collective_id=0, has_side_effects=True, vmem_limit_bytes=60 * 2**20
+            collective_id=0, has_side_effects=True, vmem_limit_bytes=54 * 2**20
         ),
         cost_estimate=pl.CostEstimate(
             flops=6 * 8 * PAIR * LANES * D, bytes_accessed=6 * ROWS * D * 2, transcendentals=8 * PAIR * LANES

time: 75.8 us -> 74 us (0.976)
  Pallas kernels: 71 us -> 68.7 us
    pallas_call x1, Pallas kernels: 71 us -> 68.7 us  [per_device(): pl.pallas_call(kernel, out_shape=(wide, wide), in_specs=[vmem, vmem, hbm,...]
where the time goes in v4:
time: 74 us; the launch traced here: 73.3 us
  Pallas kernels  68.7 us (93%)
  other arithmetic  2.65 us (4%)
  between operations  1.97 us (3%)
    pallas_call x1, Pallas kernels, per_device(): pl.pallas_call(kernel, out_shape=(wide, wide), in_specs=[vmem, vmem, hbm,...  68.7 us
    mul x1, other arithmetic, per_device(): return (image_sum * half_scale, text_sum * half_scale)  2.65 us

profile of v4, /device:TPU:1, one launch (start us, length us, event | category | flops | bytes accessed | tf_op | source)
XLA Modules:
  0.0 73.3 jit_solution(10761108452723088627)
XLA Ops:
  2.0 68.7 %shard_map.59 = (f32[176,1152]{1,0:T(8,128)}, f32[176,1152]{1,0:T(8,128)}) custom-call(f32[1,1]{1,0:T(1,128)} %bitcast.3.scale_ref, f32[1,1]{1,0:T(1,128)} %bitcast.4.offset_ref, bf16[176,1152]{1,0:T(8,128)(2,1)} %picture_ref.1, bf16[176,1152]{1,0:T(8,128)(2,1)} %caption_ref.1), custom_call_target="tpu_custom_call" | custom-call | flops 27405582336 | bytes 2433024 | tf_op jit(solution)/shard_map/pallas_call | solution.py:354
  70.7 2.7 %broadcast_multiply_fusion = (f32[176,1152]{1,0:T(8,128)}, f32[176,1152]{1,0:T(8,128)}) fusion(f32[176,1152]{1,0:T(8,128)} %get-tuple-element.5, f32[]{:T(128)} %bitcast.2, f32[176,1152]{1,0:T(8,128)} %get-tuple-element.4), kind=kLoop, calls=%fused_computation | loop fusion | flops 405504 | bytes 3244036 | tf_op jit(solution)/shard_map/mul | solution.py:391

commit v5 on v4

--- a/solution.py
+++ b/solution.py
@@ -254,68 +254,49 @@
     arrive(1)
     arrive(2)
     twin(1).wait_recv()
-    scores(0, PAIR, PAIR, tiles(128))
-    scores(PAIR, PAIR, PAIR, tiles(128))
+    scores(0, 2 * PAIR, 2 * PAIR, tiles(128))
     arrive(3)
-    scores(0, PAIR, PAIR, ((128, 384),))
-    scores(0, PAIR, PAIR, ((384, 640),))
-    scores(PAIR, PAIR, PAIR, ((128, 384),))
+    scores(0, 2 * PAIR, 2 * PAIR, ((128, 384),))
+    scores(0, 2 * PAIR, 2 * PAIR, ((384, 640),))
     twin(2).wait_recv()
-    scores(2 * PAIR, PAIR, PAIR, tiles(384))
-    scores(2 * PAIR, PAIR, PAIR, ((384, 640),))
+    scores(2 * PAIR, PAIR, PAIR, tiles(640))
     image_terms(2, 640)
     arrive(4)
-    scores(PAIR, PAIR, PAIR, ((384, 640),))
     text_terms(128, 384, 1024)
     twin(3).wait_recv()
     scores(3 * PAIR, PAIR, PAIR, tiles(640))
     image_terms(3, 640)
     arrive(5)
     twin(4).wait_recv()
-    scores(2 * PAIR, PAIR, PAIR, ((640, 896),))
     scores(4 * PAIR, PAIR, PAIR, tiles(640))
-    scores(4 * PAIR, PAIR, PAIR, ((640, 896),))
-    scores(3 * PAIR, PAIR, PAIR, ((640, 896),))
-    scores(PAIR, PAIR, PAIR, ((640, 896),))
-    scores(0, PAIR, PAIR, ((640, 896),))
+    scores(0, 5 * PAIR, 880, ((640, 896),))
     twin(5).wait_recv()
     scores(5 * PAIR, PAIR, PAIR, tiles(896))
     arrive(6)
-    scores(4 * PAIR, PAIR, PAIR, ((896, 1152),))
+    scores(0, 6 * PAIR, 704, ((896, 1152),))
     arrive(7)
-    scores(5 * PAIR, PAIR, PAIR, ((1152, 1408),))
-    scores(0, PAIR, PAIR, ((896, 1152),))
-    scores(2 * PAIR, PAIR, PAIR, ((896, 1152),))
-    scores(2 * PAIR, PAIR, PAIR, ((1152, 1408),))
-    scores(PAIR, PAIR, PAIR, ((1152, 1408),))
-    scores(0, PAIR, PAIR, ((1152, 1408),))
-    scores(3 * PAIR, PAIR, PAIR, ((1152, 1408),))
     twin(6).wait_recv()
-    scores(6 * PAIR, PAIR, PAIR, tiles(1152))
-    scores(5 * PAIR, PAIR, PAIR, ((896, 1152),))
-    scores(6 * PAIR, PAIR, PAIR, ((1152, 1408),))
+    scores(6 * PAIR, PAIR, PAIR, tiles(1408))
     image_terms(6)
+    scores(0, 6 * PAIR, 704, ((1152, 1408),))
     twin(7).wait_recv()
-    scores(4 * PAIR, PAIR, PAIR, ((1152, 1408),))
     scores(7 * PAIR, PAIR, PAIR, ((1152, 1408),))
-    scores(PAIR, PAIR, PAIR, ((896, 1152),))
+    finish(IMG, 6)
     text_terms(1152, 1408)
-    finish(IMG, 6)
+    finish(TXT, 7)
     scores(7 * PAIR, PAIR, PAIR, tiles(1152))
-    finish(TXT, 7)
     image_terms(7)
-    scores(3 * PAIR, PAIR, PAIR, ((896, 1152),))
-    image_terms(3)
     text_terms(896, 1152)
     finish(IMG, 7)
     finish(TXT, 6)
     image_terms(5)
-    finish(IMG, 3)
     text_terms(640, 896)
     finish(TXT, 4)
     finish(TXT, 5)
+    finish(IMG, 5)
+    image_terms(3)
     image_terms(4)
-    finish(IMG, 5)
+    finish(IMG, 3)
     text_terms(384, 640)
     image_terms(2)
     finish(TXT, 3)

time: 74 us -> 74.8 us (1.011)
  Pallas kernels: 68.7 us -> 70 us
    pallas_call x1, Pallas kernels: 68.7 us -> 70 us  [per_device(): pl.pallas_call(kernel, out_shape=(wide, wide), in_specs=[vmem, vmem, hbm,...]
where the time goes in v5:
time: 74.8 us; the launch traced here: 74.6 us
  Pallas kernels  70 us (94%)
  other arithmetic  2.65 us (4%)
  between operations  1.97 us (3%)
    pallas_call x1, Pallas kernels, per_device(): pl.pallas_call(kernel, out_shape=(wide, wide), in_specs=[vmem, vmem, hbm,...  70 us
    mul x1, other arithmetic, per_device(): return (image_sum * half_scale, text_sum * half_scale)  2.65 us

profile of v5, /device:TPU:1, one launch (start us, length us, event | category | flops | bytes accessed | tf_op | source)
XLA Modules:
  0.0 74.6 jit_solution(14121908978562090394)
XLA Ops:
  2.0 70.0 %shard_map.59 = (f32[176,1152]{1,0:T(8,128)}, f32[176,1152]{1,0:T(8,128)}) custom-call(f32[1,1]{1,0:T(1,128)} %bitcast.3.scale_ref, f32[1,1]{1,0:T(1,128)} %bitcast.4.offset_ref, bf16[176,1152]{1,0:T(8,128)(2,1)} %picture_ref.1, bf16[176,1152]{1,0:T(8,128)(2,1)} %caption_ref.1), custom_call_target="tpu_custom_call" | custom-call | flops 27405582336 | bytes 2433024 | tf_op jit(solution)/shard_map/pallas_call | solution.py:335
  72.0 2.7 %broadcast_multiply_fusion = (f32[176,1152]{1,0:T(8,128)}, f32[176,1152]{1,0:T(8,128)}) fusion(f32[176,1152]{1,0:T(8,128)} %get-tuple-element.5, f32[]{:T(128)} %bitcast.2, f32[176,1152]{1,0:T(8,128)} %get-tuple-element.4), kind=kLoop, calls=%fused_computation | loop fusion | flops 405504 | bytes 3244036 | tf_op jit(solution)/shard_map/mul | solution.py:372
